TPU v7x, 256 devices: a whole 4x4x8 slice. The times are simulated.
256 devices in a mesh: px: 16 (over y, x), py: 8 (over z), pair: 2 (over core).
Axes of the slice: x: 4, y: 4, z: 8, core: 2. Of those that a mesh axis runs over, the one named last changes fastest.
Arguments:
- fields: bfloat16 [2, 64, 64, 64, 128], P('pair', None, 'px', 'py'), may hold values from -6 to 6
- cotangent: bfloat16 [2, 64, 64, 64, 128], P('pair', None, 'px', 'py'), may hold values from -6 to 6
- spectral_weight: bfloat16 [16, 16, 16, 64, 128], P('px', 'py'), may hold values from -0.5 to 0.5
- local_weight: bfloat16 [64, 64], replicated, may hold values from -0.75 to 0.75
- bias_term: float32 [64], replicated, may hold values from -1 to 1
Outputs:
- activation: bfloat16 [2, 64, 64, 64, 128], P('pair', None, 'px', 'py')
- input_grad: bfloat16 [2, 64, 64, 64, 128], P('pair', None, 'px', 'py')
- weight_grad: float32 [16, 16, 16, 64, 128], P('px', 'py')
All inputs are finite; a program needn't handle non-finite values.
Results may differ from a plain program's by a relative error of at most 0.0053.
Values sent between devices are 32-bit elements; how exact they have to be, the bound alone decides.
No kernel may reach another device: no remote copies, remote signals or barrier semaphores. Data moves between devices by JAX's collectives and lax.ppermute only.
A program may use at most 64 MiB of HBM per device.

v0:
```python
import math

import jax
import jax.numpy as jnp
import ml_dtypes
import numpy as np
from jax import lax
from jax.experimental import pallas as pl
from jax.experimental.pallas import tpu as pltpu
from jax.sharding import PartitionSpec as P

C = 64
KX = 16
KY = 16
KZ = 16
NX = 64
NY = 64
NZ = 128
PX = 16
PY = 8
CELLS = 32
MODES = 32
FORWARD_FACTOR = 1.0 / math.sqrt(NX * NY * NZ)
INVERSE_FACTOR = 1.0 / math.sqrt(KX * KY * KZ)
F32 = jnp.float32
BF16 = jnp.bfloat16


def cos_sin(cells, modes, length):
    phases = np.outer(np.arange(cells), np.arange(modes)) % length
    angles = phases * (2.0 * math.pi / length)
    return np.cos(angles), np.sin(angles)


def halves(table):
    table = table.astype(np.float32)
    high = table.astype(ml_dtypes.bfloat16)
    low = (table - high.astype(np.float32)).astype(ml_dtypes.bfloat16)
    return high, low


def stacked_table(table, axis):
    high, low = halves(table)
    return np.concatenate([high, high, low], axis=axis)


def depth_tables():
    cosine, sine = cos_sin(NZ, KZ, NZ)
    order = np.arange(KZ).reshape(PY, KZ // PY).T.reshape(-1)
    forward = np.concatenate([cosine.T[order], -sine.T[order]], axis=0)
    backward = np.concatenate([cosine.T[order], -sine.T[order]], axis=0)
    forward = forward.astype(np.float32).astype(ml_dtypes.bfloat16)
    return forward, stacked_table(backward, 0)


def second_tables():
    cosine, sine = cos_sin(NY, KY, NY)
    forward = np.concatenate([cosine.T, sine.T], axis=0)
    backward = np.concatenate([cosine, sine], axis=1)
    return stacked_table(forward, 1), stacked_table(backward, 1)


def first_tables():
    cosine, sine = cos_sin(NX, KX, NX)
    by_x = [cosine.reshape(PX, 2, 2, KX), sine.reshape(PX, 2, 2, KX)]
    table = np.zeros((2, 2, 2, KX, PX, 2, 2, 2))
    for kz in range(2):
        turned = [np.transpose(t, (2, 3, 0, 1)) for t in by_x]
        table[:, 0, kz, :, :, 0, kz, :] = turned[0]
        table[:, 0, kz, :, :, 1, kz, :] = turned[1]
        table[:, 1, kz, :, :, 0, kz, :] = -turned[1]
        table[:, 1, kz, :, :, 1, kz, :] = turned[0]
    table = table.reshape(128, 128)
    return stacked_table(table, 1), stacked_table(table.T, 1)


def stacked(values):
    high = values.astype(BF16)
    low = (values - high.astype(F32)).astype(BF16)
    return jnp.concatenate([high, low, high], axis=0)


def dot(left, right):
    return jnp.dot(left, right, preferred_element_type=F32)


def dot_lanes(left, right):
    return lax.dot_general(left, right, (((1,), (1,)), ((), ())), preferred_element_type=F32)


def dot_rows(left, right, precision=None):
    return lax.dot_general(
        left, right, (((0,), (0,)), ((), ())), preferred_element_type=F32, precision=precision
    )


def call(body, outs, name, scratch=(), flops=0, nbytes=0):
    return pl.pallas_call(
        body,
        out_shape=outs,
        scratch_shapes=list(scratch),
        compiler_params=pltpu.CompilerParams(vmem_limit_bytes=24 * 1024 * 1024),
        cost_estimate=pl.CostEstimate(flops=flops, bytes_accessed=nbytes, transcendentals=0),
        name=name,
    )


def shape(rows, dtype=F32, lanes=128):
    return jax.ShapeDtypeStruct((rows, lanes), dtype)


def cell_pair(wide, y, pair):
    parts = [wide[pl.ds((2 * pair + q) * 8 + y, C, stride=CELLS), :] for q in range(2)]
    return jnp.concatenate(parts, axis=0)


def put_cell_pair(wide, y, pair, values):
    for q in range(2):
        wide[pl.ds((2 * pair + q) * 8 + y, C, stride=CELLS), :] = values[q * C : (q + 1) * C]


def pair_rows(y, pair):
    return pl.ds(pl.multiple_of((y * 2 + pair) * 128, 128), 128)


def send_depth(table, cells, out_ref, y, pair):
    modes = dot_lanes(table, cells)
    for g in range(4):
        out_ref[pl.ds((g * 2 + pair) * 8 + y, PY, stride=64), :] = modes[g * 8 : (g + 1) * 8]


def depth_modes(ref, y, pair):
    parts = [ref[pl.ds((g * 2 + pair) * 8 + y, PY, stride=64), :] for g in range(4)]
    return jnp.concatenate(parts, axis=0)


def depth_body(fields_ref, table_ref, pairs_ref, out_ref, wide):
    wide[...] = fields_ref[...].astype(F32)
    table = table_ref[...]

    def step(y, carry):
        for pair in range(2):
            cells = cell_pair(wide, y, pair).astype(BF16)
            pairs_ref[pair_rows(y, pair), :] = cells
            send_depth(table, cells, out_ref, y, pair)
        return carry

    lax.fori_loop(0, 8, step, 0)


def local_body(pairs_ref, cotangent_ref, weight_ref, bias_ref, local_ref, cot_ref, wide):
    wide[...] = cotangent_ref[...].astype(F32)
    weight = weight_ref[...]
    bias = bias_ref[...]

    def step(y, carry):
        for pair in range(2):
            rows = pair_rows(y, pair)
            cells = pairs_ref[rows, :]
            both = [dot(weight, cells[q * C : (q + 1) * C]) + bias for q in range(2)]
            local_ref[rows, :] = jnp.concatenate(both, axis=0)
            cot_ref[rows, :] = cell_pair(wide, y, pair).astype(BF16)
        return carry

    lax.fori_loop(0, 8, step, 0)


def second_forward_body(in_ref, table_ref, out_ref):
    table = table_ref[...]
    turned = []
    for lb in range(8):
        column = in_ref[:, lb * 8 : (lb + 1) * 8, :].reshape(NY, 128)
        turned.append(dot(table, stacked(column)))
    for lb in range(4):
        real, imag = turned[lb], turned[lb + 4]
        out_ref[pl.ds(lb, KY, stride=8), :] = real[:KY] + imag[KY:]
        out_ref[pl.ds(lb + 4, KY, stride=8), :] = imag[:KY] - real[KY:]


def second_inverse_body(in_ref, table_ref, out_ref):
    table = table_ref[...]
    columns = [in_ref[pl.ds(lb, KY, stride=8), :] for lb in range(8)]
    for lb in range(4):
        real, imag = columns[lb], columns[lb + 4]
        one = dot(table, stacked(jnp.concatenate([real, -imag], axis=0)))
        two = dot(table, stacked(jnp.concatenate([imag, real], axis=0)))
        out_ref[:, lb * 8 : (lb + 1) * 8, :] = one.reshape(PY, 8, 128)
        out_ref[:, (lb + 4) * 8 : (lb + 5) * 8, :] = two.reshape(PY, 8, 128)


def low_lanes(values):
    lane = lax.broadcasted_iota(jnp.int32, values.shape, 1)
    return jnp.where(lane < C, values, 0.0)


def swap_lanes(values):
    return pltpu.roll(values, C, 1)


def first_forward(values, table, factor):
    spread = dot(table, stacked(values))
    spectrum = spread[:64] + swap_lanes(spread[64:])
    return low_lanes(spectrum * factor)


def first_inverse(modes, table):
    low = low_lanes(modes)
    return dot(table, stacked(jnp.concatenate([low, swap_lanes(low)], axis=0)))


def put_rows(rows_ref, index, values):
    rows_ref[pl.ds(index, MODES, stride=8), :] = values


def get_rows(rows_ref, index):
    return rows_ref[pl.ds(index, MODES, stride=8), :]


def put_halves(rows_ref, real, imag):
    for index, values in enumerate((real, imag)):
        high = values.astype(BF16).astype(F32)
        put_rows(rows_ref, index, high)
        put_rows(rows_ref, index + 2, values - high)


def mix_body(in_ref, weight_ref, table_ref, back_ref, out_ref, spectrum_ref, rows_ref, mixed_ref):
    spectrum = first_forward(in_ref[...], table_ref[...], FORWARD_FACTOR)
    spectrum_ref[...] = spectrum
    rows_ref[...] = jnp.zeros_like(rows_ref)
    put_halves(rows_ref, spectrum[:MODES], spectrum[MODES:])
    for m in range(MODES):
        rows = rows_ref[m * 8 : (m + 1) * 8, :].astype(BF16)
        mixed_ref[m * 8 : (m + 1) * 8, :] = dot(rows[:, :C], weight_ref[m * C : (m + 1) * C, :])
    by_real = get_rows(mixed_ref, 0) + get_rows(mixed_ref, 2)
    by_imag = get_rows(mixed_ref, 1) + get_rows(mixed_ref, 3)
    mixed = jnp.concatenate(
        [by_real - swap_lanes(by_imag), swap_lanes(by_real) + by_imag], axis=0
    )
    out_ref[...] = first_inverse(mixed * INVERSE_FACTOR, back_ref[...])


def both_columns(spectrum):
    real, imag = spectrum[:MODES], spectrum[MODES:]
    return real + swap_lanes(imag), imag - swap_lanes(real)


def mix_back_body(
    in_ref, weight_ref, spectrum_ref, table_ref, back_ref, out_ref, pack_ref, rows_ref, mixed_ref
):
    grad_spec = first_forward(in_ref[...], table_ref[...], INVERSE_FACTOR)
    pack_ref[0:64, :] = spectrum_ref[...]
    pack_ref[64:128, :] = grad_spec
    straight, turned = both_columns(grad_spec)
    rows_ref[...] = jnp.zeros_like(rows_ref)
    put_halves(rows_ref, straight, turned)
    mixed_ref[...] = jnp.zeros_like(mixed_ref)
    for m in range(MODES):
        rows = rows_ref[m * 8 : (m + 1) * 8, :].astype(BF16)
        mixed_ref[m * 8 : (m + 1) * 8, :C] = dot_lanes(rows, weight_ref[m * C : (m + 1) * C, :])
    real = get_rows(mixed_ref, 0) + get_rows(mixed_ref, 2)
    imag = get_rows(mixed_ref, 1) + get_rows(mixed_ref, 3)
    modes = jnp.concatenate([real, imag], axis=0)
    out_ref[...] = first_inverse(modes * FORWARD_FACTOR, back_ref[...])


def weight_grad_body(mine_ref, other_ref, out_ref, left_ref, right_ref):
    left_ref[...] = jnp.zeros_like(left_ref)
    right_ref[...] = jnp.zeros_like(right_ref)
    for index, pack_ref in enumerate((mine_ref, other_ref)):
        straight, turned = both_columns(pack_ref[64:128, :])
        put_rows(left_ref, 2 * index, pack_ref[0:MODES, :])
        put_rows(left_ref, 2 * index + 1, pack_ref[MODES : 2 * MODES, :])
        put_rows(right_ref, 2 * index, straight)
        put_rows(right_ref, 2 * index + 1, turned)
    for m in range(MODES):
        rows = slice(m * 8, (m + 1) * 8)
        out_ref[m * C : (m + 1) * C, :] = dot_rows(
            left_ref[rows, :], right_ref[rows, :], lax.Precision.HIGHEST
        )[:C]


ERFC = (
    0.17087277,
    -0.82215223,
    1.48851587,
    -1.13520398,
    0.27886807,
    -0.18628806,
    0.09678418,
    0.37409196,
    1.00002368,
    -1.26551223,
)


def gelu_and_slope(pre):
    bell = jnp.exp(-0.5 * pre * pre)
    t = 1.0 / (1.0 + (0.5 / math.sqrt(2.0)) * jnp.abs(pre))
    series = jnp.full_like(t, ERFC[0])
    for coefficient in ERFC[1:]:
        series = series * t + coefficient
    tail = (0.5 * t) * (jnp.exp(series) * bell)
    cumulative = jnp.where(pre < 0.0, tail, 1.0 - tail)
    return pre * cumulative, cumulative + pre * (bell * (1.0 / math.sqrt(2.0 * math.pi)))


def middle_body(
    in_ref, local_ref, cot_ref, back_ref, table_ref, act_ref, grad_ref, out_ref, wide
):
    back = back_ref[...]
    table = table_ref[...]

    def step(y, carry):
        for pair in range(2):
            rows = pair_rows(y, pair)
            pre = local_ref[rows, :] + dot_rows(stacked(depth_modes(in_ref, y, pair)), back)
            activation, slope = gelu_and_slope(pre)
            put_cell_pair(wide, y, pair, activation)
            grad_pre = (cot_ref[rows, :].astype(F32) * slope).astype(BF16)
            grad_ref[rows, :] = grad_pre
            send_depth(table, grad_pre, out_ref, y, pair)
        return carry

    lax.fori_loop(0, 8, step, 0)
    act_ref[...] = wide[...].astype(BF16)


def last_body(in_ref, grad_ref, weight_ref, back_ref, out_ref, wide):
    back = back_ref[...]
    weight = weight_ref[...]

    def step(y, carry):
        for pair in range(2):
            cells = grad_ref[pair_rows(y, pair), :]
            both = [dot(weight, cells[q * C : (q + 1) * C]) for q in range(2)]
            total = jnp.concatenate(both, axis=0)
            total += dot_rows(stacked(depth_modes(in_ref, y, pair)), back)
            put_cell_pair(wide, y, pair, total)
        return carry

    lax.fori_loop(0, 8, step, 0)
    out_ref[...] = wide[...].astype(BF16)


def over_py(values):
    return lax.all_to_all(values.reshape(PY, 64, 128), "py", 0, 0, tiled=True)


def over_px(values):
    return lax.all_to_all(values.reshape(PX, 8, 128), "px", 0, 0, tiled=True).reshape(128, 128)


def shards(fields, cotangent, spectral_weight, local_weight, bias_term):
    depth_table, depth_back = depth_tables()
    second_table, second_back = second_tables()
    first_table, first_back = first_tables()
    weight = spectral_weight.reshape(MODES * C, 128)
    wide = pltpu.VMEM((C * CELLS, 128), F32)
    rows = pltpu.VMEM((MODES * 8, 128), F32)
    cells = C * CELLS
    second_forward = call(second_forward_body, shape(128), "y_forward")
    second_inverse = call(
        second_inverse_body, jax.ShapeDtypeStruct((PY, 64, 128), F32), "y_inverse"
    )

    pairs, sent = call(depth_body, (shape(cells, BF16), shape(512)), "z_forward", [wide])(
        fields.reshape(cells, 128), depth_table
    )
    received = over_py(sent)
    local, cot = call(
        local_body,
        (shape(cells), shape(cells, BF16)),
        "local_mix",
        [wide],
        flops=2 * C * cells * 128,
        nbytes=5 * cells * 256,
    )(
        pairs,
        cotangent.reshape(cells, 128),
        jnp.transpose(local_weight),
        bias_term.reshape(C, 1),
    )
    received = over_px(second_forward(received, second_table))
    sent, spectrum = call(mix_body, (shape(128), shape(64)), "modes_mix", [rows, rows])(
        received, weight, first_table, first_back
    )
    received = over_py(second_inverse(over_px(sent), second_back))
    activation, grad_pre, sent = call(
        middle_body,
        (shape(cells, BF16), shape(cells, BF16), shape(512)),
        "gelu_z",
        [wide],
    )(received.reshape(512, 128), local, cot, depth_back, depth_table)
    received = over_px(second_forward(over_py(sent), second_table))
    sent, pack = call(mix_back_body, (shape(128), shape(128)), "modes_back", [rows, rows])(
        received, weight, spectrum, first_table, first_back
    )
    received = over_px(sent)
    other = lax.ppermute(pack, "pair", [(0, 1), (1, 0)])
    weight_grad = call(
        weight_grad_body, shape(MODES * C), "weight_grad", [rows, rows], flops=10**8, nbytes=10**6
    )(pack, other)
    received = over_py(second_inverse(received, second_back))
    input_grad = call(last_body, shape(cells, BF16), "z_inverse", [wide])(
        received.reshape(512, 128), grad_pre, local_weight, depth_back
    )
    return (
        activation.reshape(fields.shape),
        input_grad.reshape(fields.shape),
        weight_grad.reshape(spectral_weight.shape),
    )


def solution(mesh):
    grid = P("pair", None, "px", "py", None)
    modes = P("px", "py", None, None, None)
    return jax.shard_map(
        shards,
        mesh=mesh,
        in_specs=(grid, grid, modes, P(), P()),
        out_specs=(grid, grid, modes),
        check_vma=False,
    )
```

profile of v0, /device:TPU:2, one launch (start us, length us, event | category | flops | bytes accessed | tf_op | source)
XLA Modules:
  0.0 125.8 jit_solution(14773748722361959687)
XLA Ops:
  0.6 0.0 copy-start.13
  0.6 0.7 copy-done.13
  1.3 0.0 copy-start.1
  1.3 1.0 copy-done.1
  2.4 0.0 copy-start.11
  2.4 1.8 %z_forward.1 = (bf16[2048,128]{1,0:T(8,128)(2,1)S(1)}, f32[512,128]{1,0:T(8,128)S(1)}) custom-call(bf16[2048,128]{1,0:T(8,128)(2,1)S(1)} %bitcast.24, bf16[32,128]{1,0:T(8,128)(2,1)S(1)} %copy-done.13), custom_call_target="tpu_custom_call" | custom-call | tf_op jit(solution)/shard_map/z_forward/pallas_call | solution.py:366
  4.2 0.0 copy-start
  4.2 20.3 %all_to_all.40.in_ref = f32[8,64,128]{2,1,0:T(8,128)S(1)} all-to-all(f32[8,64,128]{2,1,0:T(8,128)S(1)} %bitcast.29), channel_id=1, replica_groups=mesh['px'=16,'py'=8,'pair'=2] {'py'}, dimensions={0} | all-to-all | bytes 524288 | tf_op jit(solution)/shard_map/all_to_all | solution.py:346
  24.4 0.0 copy-done.11
  24.4 0.0 copy-start.4
  24.4 0.2 y_forward.2
  24.7 0.0 copy-start.3
  24.7 13.7 %all_to_all.41 = f32[16,8,128]{2,1,0:T(8,128)S(1)} all-to-all(f32[16,8,128]{2,1,0:T(8,128)S(1)} %bitcast.32), channel_id=1, replica_groups=mesh['px'=16,'py'=8,'pair'=2] {'px'}, dimensions={0} | all-to-all | bytes 131072 | tf_op jit(solution)/shard_map/all_to_all | solution.py:350
  38.4 0.0 copy-done
  38.4 0.0 copy-done.4
  38.4 0.0 copy-done.3
  38.4 0.0 copy-start.9
  38.4 0.8 modes_mix.1
  39.3 0.0 copy-start.15
  39.3 0.0 copy-start.2
  39.3 10.9 %all_to_all.42 = f32[16,8,128]{2,1,0:T(8,128)S(1)} all-to-all(f32[16,8,128]{2,1,0:T(8,128)S(1)} %bitcast.36), channel_id=1, replica_groups=mesh['px'=16,'py'=8,'pair'=2] {'px'}, dimensions={0} | all-to-all | bytes 131072 | tf_op jit(solution)/shard_map/all_to_all | solution.py:350
  50.2 0.0 copy-done.15
  50.2 0.0 copy-done.9
  50.2 0.9 y_inverse.2
  51.1 0.0 copy-start.7
  51.1 3.5 %all-to-all-start.3 = ((f32[8,64,128]{2,1,0:T(8,128)}), f32[8,64,128]{2,1,0:T(8,128)S(1)}, u32[]{:S(2)}, u32[]{:S(2)}) async-start(f32[8,64,128]{2,1,0:T(8,128)} %y_inverse.2), calls=%async_computation.3 | async-start | bytes 524288 | tf_op jit(solution)/shard_map/all_to_all | solution.py:346
  54.7 0.0 copy-done.7
  54.7 0.7 copy.14
  55.4 0.0 copy-start.17
  55.4 0.7 copy-done.17
  56.0 0.1 copy.15.bias_ref
  56.1 0.0 copy-done.2
  56.1 0.0 copy-start.8
  56.2 0.7 copy-done.8
  56.9 1.9 %local_mix.1 = (f32[2048,128]{1,0:T(8,128)S(1)}, bf16[2048,128]{1,0:T(8,128)(2,1)S(1)}) custom-call(bf16[2048,128]{1,0:T(8,128)(2,1)S(1)} %get-tuple-element.16.pairs_ref, bf16[2048,128]{1,0:T(8,128)(2,1)S(1)} %bitcast.25, bf16[64,64]{1,0:T(8,128)(2,1)S(1)} %bitcast.34, f32[64,1]{1,0:T(8,128)S(1)} %copy.15.bias_ref), custom_call_target="tpu_custom_call" | custom-call | flops 33554432 | bytes 2621440 | tf_op jit(solution)/shard_map/local_mix/pallas_call | solution.py:370
  58.8 6.3 %all-to-all-done.3 = f32[8,64,128]{2,1,0:T(8,128)S(1)} async-done(((f32[8,64,128]{2,1,0:T(8,128)}), f32[8,64,128]{2,1,0:T(8,128)S(1)}, u32[]{:S(2)}, u32[]{:S(2)}) %all-to-all-start.3) | async-done | bytes 262176 | tf_op jit(solution)/shard_map/all_to_all | solution.py:346
  65.1 0.0 copy-start.6
  65.1 0.7 copy-done.6
  65.8 0.0 copy-start.14
  65.8 0.7 copy-done.14
  66.5 5.5 %gelu_z.1 = (bf16[2048,128]{1,0:T(8,128)(2,1)}, bf16[2048,128]{1,0:T(8,128)(2,1)S(1)}, f32[512,128]{1,0:T(8,128)S(1)}) custom-call(f32[512,128]{1,0:T(8,128)S(1)} %bitcast.22, f32[2048,128]{1,0:T(8,128)S(1)} %get-tuple-element.17.local_ref, bf16[2048,128]{1,0:T(8,128)(2,1)S(1)} %get-tuple-element.18.cot_ref, bf16[96,128]{1,0:T(8,128)(2,1)S(1)} %copy-done.6, ...), custom_call_target="tpu_custom_call" | custom-call | tf_op jit(solution)/shard_map/gelu_z/pallas_call | solution.py:388
  72.0 0.0 copy-start.12
  72.0 13.0 %all_to_all.43.in_ref = f32[8,64,128]{2,1,0:T(8,128)S(1)} all-to-all(f32[8,64,128]{2,1,0:T(8,128)S(1)} %bitcast.28), channel_id=1, replica_groups=mesh['px'=16,'py'=8,'pair'=2] {'py'}, dimensions={0} | all-to-all | bytes 524288 | tf_op jit(solution)/shard_map/all_to_all | solution.py:346
  85.0 0.0 copy-done.12
  85.0 0.2 y_forward.3
  85.2 0.0 copy-start.5
  85.3 0.0 copy-start.16
  85.3 10.9 %all_to_all.44 = f32[16,8,128]{2,1,0:T(8,128)S(1)} all-to-all(f32[16,8,128]{2,1,0:T(8,128)S(1)} %bitcast.30), channel_id=1, replica_groups=mesh['px'=16,'py'=8,'pair'=2] {'px'}, dimensions={0} | all-to-all | bytes 131072 | tf_op jit(solution)/shard_map/all_to_all | solution.py:350
  96.2 0.0 copy-done.5
  96.2 0.0 copy-done.16
  96.2 0.9 modes_back.1
  97.2 0.0 copy-start.10
  97.2 10.8 %all_to_all.45 = f32[16,8,128]{2,1,0:T(8,128)S(1)} all-to-all(f32[16,8,128]{2,1,0:T(8,128)S(1)} %bitcast.35), channel_id=1, replica_groups=mesh['px'=16,'py'=8,'pair'=2] {'px'}, dimensions={0} | all-to-all | bytes 131072 | tf_op jit(solution)/shard_map/all_to_all | solution.py:350
  108.0 0.0 copy-done.10
  108.0 0.9 y_inverse.3
  108.9 3.4 %all-to-all-start.7 = ((f32[8,64,128]{2,1,0:T(8,128)}), f32[8,64,128]{2,1,0:T(8,128)S(1)}, u32[]{:S(2)}, u32[]{:S(2)}) async-start(f32[8,64,128]{2,1,0:T(8,128)} %y_inverse.3), calls=%async_computation.7 | async-start | bytes 524288 | tf_op jit(solution)/shard_map/all_to_all | solution.py:346
  112.3 0.1 collective-permute-start
  112.4 1.2 collective-permute-done.other_ref
  113.6 2.8 %weight_grad.1 = f32[2048,128]{1,0:T(8,128)} custom-call(f32[128,128]{1,0:T(8,128)S(1)} %get-tuple-element.24.mine_ref, f32[128,128]{1,0:T(8,128)S(1)} %collective-permute-done.other_ref), custom_call_target="tpu_custom_call" | custom-call | flops 100000000 | bytes 1000000 | tf_op jit(solution)/shard_map/weight_grad/pallas_call | solution.py:400
  116.5 6.2 %all-to-all-done.7 = f32[8,64,128]{2,1,0:T(8,128)S(1)} async-done(((f32[8,64,128]{2,1,0:T(8,128)}), f32[8,64,128]{2,1,0:T(8,128)S(1)}, u32[]{:S(2)}, u32[]{:S(2)}) %all-to-all-start.7) | async-done | bytes 262176 | tf_op jit(solution)/shard_map/all_to_all | solution.py:346
  122.7 3.1 %z_inverse.1 = bf16[2048,128]{1,0:T(8,128)(2,1)} custom-call(f32[512,128]{1,0:T(8,128)S(1)} %bitcast.23, bf16[2048,128]{1,0:T(8,128)(2,1)S(1)} %get-tuple-element.23.grad_ref, bf16[64,64]{1,0:T(8,128)(2,1)S(1)} %copy-done.7, bf16[96,128]{1,0:T(8,128)(2,1)S(1)} %copy-done.6), custom_call_target="tpu_custom_call" | custom-call | tf_op jit(solution)/shard_map/z_inverse/pallas_call | solution.py:404
Async XLA Ops:
  0.6 0.7 copy-start.13
  1.3 1.0 copy-start.1
  2.4 22.1 %copy-start.11 = (bf16[32,192]{1,0:T(8,128)(2,1)S(1)}, bf16[32,192]{1,0:T(8,128)(2,1)}, u32[]{:S(2)}) copy-start(bf16[32,192]{1,0:T(8,128)(2,1)} %constant.13.clone.table_ref) | copy-start | bytes 36868
  4.2 34.3 %copy-start = (bf16[1,2,16,64,128]{4,3,2,1,0:T(8,128)(2,1)S(1)}, bf16[1,2,16,64,128]{4,3,2,1,0:T(8,128)(2,1)}, u32[]{:S(2)}) copy-start(bf16[1,2,16,64,128]{4,3,2,1,0:T(8,128)(2,1)} %param.13) | copy-start | bytes 1572868
  24.4 14.0 %copy-start.4 = (bf16[128,384]{1,0:T(8,128)(2,1)S(1)}, bf16[128,384]{1,0:T(8,128)(2,1)}, u32[]{:S(2)}) copy-start(bf16[128,384]{1,0:T(8,128)(2,1)} %constant.14.clone.table_ref) | copy-start | bytes 294916
  24.7 13.7 %copy-start.3 = (bf16[128,384]{1,0:T(8,128)(2,1)S(1)}, bf16[128,384]{1,0:T(8,128)(2,1)}, u32[]{:S(2)}) copy-start(bf16[128,384]{1,0:T(8,128)(2,1)} %constant.15.clone.back_ref) | copy-start | bytes 294916
  38.4 11.8 %copy-start.9 = (bf16[64,96]{1,0:T(8,128)(2,1)S(1)}, bf16[64,96]{1,0:T(8,128)(2,1)}, u32[]{:S(2)}) copy-start(bf16[64,96]{1,0:T(8,128)(2,1)} %constant.16.clone.table_ref) | copy-start | bytes 36868
  39.3 11.0 %copy-start.15 = (f32[64,128]{1,0:T(8,128)}, f32[64,128]{1,0:T(8,128)S(1)}, u32[]{:S(2)}) copy-start(f32[64,128]{1,0:T(8,128)S(1)} %get-tuple-element.21.spectrum_ref) | copy-start | bytes 98308
  39.3 16.9 %copy-start.2 = (bf16[1,64,4,8,128]{4,3,2,1,0:T(8,128)(2,1)S(1)}, bf16[1,64,4,8,128]{4,3,2,1,0:T(8,128)(2,1)}, u32[]{:S(2)}) copy-start(bf16[1,64,4,8,128]{4,3,2,1,0:T(8,128)(2,1)} %param.12) | copy-start | bytes 1572868
  51.1 3.6 %copy-start.7 = (bf16[64,64]{1,0:T(8,128)(2,1)S(1)}, bf16[64,64]{1,0:T(8,128)(2,1)}, u32[]{:S(2)}) copy-start(bf16[64,64]{1,0:T(8,128)(2,1)} %weight_ref.1) | copy-start | bytes 24580
  51.1 13.9 %all-to-all-start.3 = ((f32[8,64,128]{2,1,0:T(8,128)}), f32[8,64,128]{2,1,0:T(8,128)S(1)}, u32[]{:S(2)}, u32[]{:S(2)}) async-start(f32[8,64,128]{2,1,0:T(8,128)} %y_inverse.2), calls=%async_computation.3 | async-start | bytes 524288 | tf_op jit(solution)/shard_map/all_to_all | solution.py:346
  55.4 0.7 copy-start.17
  56.1 0.7 copy-start.8
  65.1 0.7 copy-start.6
  65.8 0.7 copy-start.14
  72.0 13.0 %copy-start.12 = (bf16[32,192]{1,0:T(8,128)(2,1)S(1)}, bf16[32,192]{1,0:T(8,128)(2,1)}, u32[]{:S(2)}) copy-start(bf16[32,192]{1,0:T(8,128)(2,1)} %constant.13.clone.table_ref) | copy-start | bytes 36868
  85.2 11.0 %copy-start.5 = (bf16[128,384]{1,0:T(8,128)(2,1)S(1)}, bf16[128,384]{1,0:T(8,128)(2,1)}, u32[]{:S(2)}) copy-start(bf16[128,384]{1,0:T(8,128)(2,1)} %constant.14.clone.table_ref) | copy-start | bytes 294916
  85.3 10.9 %copy-start.16 = (f32[64,128]{1,0:T(8,128)S(1)}, f32[64,128]{1,0:T(8,128)}, u32[]{:S(2)}) copy-start(f32[64,128]{1,0:T(8,128)} %copy-done.15) | copy-start | bytes 98308
  97.2 10.8 %copy-start.10 = (bf16[64,96]{1,0:T(8,128)(2,1)S(1)}, bf16[64,96]{1,0:T(8,128)(2,1)}, u32[]{:S(2)}) copy-start(bf16[64,96]{1,0:T(8,128)(2,1)} %constant.16.clone.table_ref) | copy-start | bytes 36868
  108.9 13.8 %all-to-all-start.7 = ((f32[8,64,128]{2,1,0:T(8,128)}), f32[8,64,128]{2,1,0:T(8,128)S(1)}, u32[]{:S(2)}, u32[]{:S(2)}) async-start(f32[8,64,128]{2,1,0:T(8,128)} %y_inverse.3), calls=%async_computation.7 | async-start | bytes 524288 | tf_op jit(solution)/shard_map/all_to_all | solution.py:346
  112.3 1.3 %collective-permute-start = (f32[128,128]{1,0:T(8,128)S(1)}, f32[128,128]{1,0:T(8,128)S(1)}, u32[]{:S(2)}, u32[]{:S(2)}) collective-permute-start(f32[128,128]{1,0:T(8,128)S(1)} %get-tuple-element.24.mine_ref), channel_id=1, source_target_pairs={{0,1},{1,0},{2,3},{3,2},{4,5},{5,4},{6,7},{7,6},{8,9},{9,8},{10,11... | collective-permute-start | bytes 196616 | tf_op jit(solution)/shard_map/ppermute | solution.py:399
where the time goes:
time: 127 us; the launch traced here: 126 us
  blocking collectives  79.6 us (63%)
  Pallas kernels  19.2 us (15%)
  waiting for transfers between devices  13.7 us (11%)
  starting transfers between devices  7.05 us (6%)
  local copies, waits for them, and re-layouts  5.43 us (4%)
    all_to_all x4, blocking collectives, over_px(): lax.all_to_all(values.reshape(PX, 8, 128), 'px', 0, 0, tiled=True)  46.4 us
    all_to_all x2, blocking collectives, over_py(): return lax.all_to_all(values.reshape(PY, 64, 128), 'py', 0, 0, tiled=True)  33.3 us
    all_to_all x2, waiting for transfers between devices, over_py(): return lax.all_to_all(values.reshape(PY, 64, 128), 'py', 0, 0, tiled=True)  12.5 us
    all_to_all x2, starting transfers between devices, over_py(): return lax.all_to_all(values.reshape(PY, 64, 128), 'py', 0, 0, tiled=True)  6.96 us
    pallas_call x1, Pallas kernels, shards(): call(middle_body, (shape(cells, BF16), shape(cells, BF16), shape(512)), '...  5.5 us
    unnamed x37, local copies, waits for them, and re-layouts  5.33 us
    pallas_call x1, Pallas kernels, shards(): call(last_body, shape(cells, BF16), 'z_inverse', [wide])  3.11 us
    pallas_call x1, Pallas kernels, shards(): call(weight_grad_body, shape(MODES * C), 'weight_grad', [rows, rows], flo...  2.84 us
  transfers between devices with their start and end apart: 3, of which 3 were waited for; matrix products, arithmetic and copies ran while one was open for 1% of the time, Pallas kernels for 4%

commit v1 on v0

--- a/solution.py
+++ b/solution.py
@@ -24,6 +24,8 @@
 INVERSE_FACTOR = 1.0 / math.sqrt(KX * KY * KZ)
 F32 = jnp.float32
 BF16 = jnp.bfloat16
+MIDDLE_GROUP = 1
+LAST_GROUP = 1
 
 
 def cos_sin(cells, modes, length):
@@ -74,6 +76,18 @@
     return stacked_table(table, 1), stacked_table(table.T, 1)
 
 
+def small_tables():
+    pieces = depth_tables() + second_tables()
+    rows = [np.pad(p, ((0, 0), (0, 256 - p.shape[1]))) for p in pieces]
+    return np.concatenate(rows, axis=0)
+
+
+DEPTH = (slice(0, 32), slice(0, 128))
+DEPTH_BACK = (slice(32, 128), slice(0, 128))
+SECOND = (slice(128, 160), slice(0, 192))
+SECOND_BACK = (slice(160, 224), slice(0, 96))
+
+
 def stacked(values):
     high = values.astype(BF16)
     low = (values - high.astype(F32)).astype(BF16)
@@ -94,7 +108,7 @@
     )
 
 
-def call(body, outs, name, scratch=(), flops=0, nbytes=0):
+def call(body, outs, name, scratch=(), flops=0, nbytes=0, **specs):
     return pl.pallas_call(
         body,
         out_shape=outs,
@@ -102,6 +116,7 @@
         compiler_params=pltpu.CompilerParams(vmem_limit_bytes=24 * 1024 * 1024),
         cost_estimate=pl.CostEstimate(flops=flops, bytes_accessed=nbytes, transcendentals=0),
         name=name,
+        **specs,
     )
 
 
@@ -109,64 +124,82 @@
     return jax.ShapeDtypeStruct((rows, lanes), dtype)
 
 
-def cell_pair(wide, y, pair):
-    parts = [wide[pl.ds((2 * pair + q) * 8 + y, C, stride=CELLS), :] for q in range(2)]
+def cell_pair(wide, y):
+    parts = [wide[pl.ds(q * 8 + y, C, stride=16), :] for q in range(2)]
     return jnp.concatenate(parts, axis=0)
 
 
-def put_cell_pair(wide, y, pair, values):
+def put_cell_pair(wide, y, values):
     for q in range(2):
-        wide[pl.ds((2 * pair + q) * 8 + y, C, stride=CELLS), :] = values[q * C : (q + 1) * C]
-
-
-def pair_rows(y, pair):
-    return pl.ds(pl.multiple_of((y * 2 + pair) * 128, 128), 128)
-
-
-def send_depth(table, cells, out_ref, y, pair):
+        wide[pl.ds(q * 8 + y, C, stride=16), :] = values[q * C : (q + 1) * C]
+
+
+def block(y, pair):
+    return slice(pair * 128, (pair + 1) * 128), slice(y * 128, (y + 1) * 128)
+
+
+def send_depth(table, cells, out_ref, ys, pair):
     modes = dot_lanes(table, cells)
-    for g in range(4):
-        out_ref[pl.ds((g * 2 + pair) * 8 + y, PY, stride=64), :] = modes[g * 8 : (g + 1) * 8]
-
-
-def depth_modes(ref, y, pair):
-    parts = [ref[pl.ds((g * 2 + pair) * 8 + y, PY, stride=64), :] for g in range(4)]
-    return jnp.concatenate(parts, axis=0)
-
-
-def depth_body(fields_ref, table_ref, pairs_ref, out_ref, wide):
-    wide[...] = fields_ref[...].astype(F32)
-    table = table_ref[...]
-
-    def step(y, carry):
-        for pair in range(2):
-            cells = cell_pair(wide, y, pair).astype(BF16)
-            pairs_ref[pair_rows(y, pair), :] = cells
-            send_depth(table, cells, out_ref, y, pair)
-        return carry
-
-    lax.fori_loop(0, 8, step, 0)
-
-
-def local_body(pairs_ref, cotangent_ref, weight_ref, bias_ref, local_ref, cot_ref, wide):
-    wide[...] = cotangent_ref[...].astype(F32)
-    weight = weight_ref[...]
-    bias = bias_ref[...]
-
-    def step(y, carry):
-        for pair in range(2):
-            rows = pair_rows(y, pair)
-            cells = pairs_ref[rows, :]
-            both = [dot(weight, cells[q * C : (q + 1) * C]) + bias for q in range(2)]
-            local_ref[rows, :] = jnp.concatenate(both, axis=0)
-            cot_ref[rows, :] = cell_pair(wide, y, pair).astype(BF16)
-        return carry
-
-    lax.fori_loop(0, 8, step, 0)
+    for i, y in enumerate(ys):
+        for g in range(4):
+            out_ref[pl.ds((g * 2 + pair) * 8 + y, PY, stride=64), :] = modes[
+                g * 8 : (g + 1) * 8, i * 128 : (i + 1) * 128
+            ]
+
+
+def depth_modes(ref, ys, pair):
+    def one(y, g):
+        return ref[pl.ds((g * 2 + pair) * 8 + y, PY, stride=64), :]
+
+    return jnp.concatenate(
+        [jnp.concatenate([one(y, g) for y in ys], axis=1) for g in range(4)], axis=0
+    )
+
+
+def back_and_local(in_ref, back, weight, cells_ref, ys, pair):
+    total = dot_rows(stacked(depth_modes(in_ref, ys, pair)), back)
+    rows = slice(pair * 128, (pair + 1) * 128)
+    mixed = dot(weight, cells_ref[rows, ys[0] * 128 : (ys[-1] + 1) * 128])
+    parts = [mixed[:, i * 128 : (i + 1) * 128] for i in range(len(ys))]
+    return total + jnp.concatenate(parts, axis=0)
+
+
+def both_cells(weight):
+    zero = jnp.zeros_like(weight)
+    return jnp.concatenate(
+        [jnp.concatenate([weight, zero], axis=1), jnp.concatenate([zero, weight], axis=1)], axis=0
+    ).astype(BF16)
+
+
+def y_groups(size):
+    return [list(range(first, first + size)) for first in range(0, 8, size)]
+
+
+def part_of(ref, pair):
+    return ref.at[:, pl.ds(pair * 16, 16), :]
+
+
+def depth_table_here():
+    row = lax.broadcasted_iota(jnp.int32, (32, 128), 0)
+    cell = lax.broadcasted_iota(jnp.int32, (32, 128), 1)
+    wave = 2 * (row % 8) + (row // 8) % 2
+    phase = (wave * cell + (NZ // 4) * (row // 16)) % NZ
+    return jnp.cos(phase.astype(F32) * (2.0 * math.pi / NZ)).astype(BF16)
+
+
+def depth_body(fields_ref, pairs_ref, out_ref, wide):
+    table = depth_table_here()
+    for pair in range(2):
+        part = fields_ref[:, pair * 16 : (pair + 1) * 16, :]
+        wide[...] = part.astype(F32).reshape(C * 16, 128)
+        for y in range(8):
+            cells = cell_pair(wide, y).astype(BF16)
+            pairs_ref[block(y, pair)] = cells
+            send_depth(table, cells, out_ref, [y], pair)
 
 
 def second_forward_body(in_ref, table_ref, out_ref):
-    table = table_ref[...]
+    table = table_ref[SECOND]
     turned = []
     for lb in range(8):
         column = in_ref[:, lb * 8 : (lb + 1) * 8, :].reshape(NY, 128)
@@ -178,7 +211,7 @@
 
 
 def second_inverse_body(in_ref, table_ref, out_ref):
-    table = table_ref[...]
+    table = table_ref[SECOND_BACK]
     columns = [in_ref[pl.ds(lb, KY, stride=8), :] for lb in range(8)]
     for lb in range(4):
         real, imag = columns[lb], columns[lb + 4]
@@ -223,7 +256,13 @@
         put_rows(rows_ref, index + 2, values - high)
 
 
-def mix_body(in_ref, weight_ref, table_ref, back_ref, out_ref, spectrum_ref, rows_ref, mixed_ref):
+def mix_body(
+    in_ref, weight_ref, table_ref, back_ref, local_ref, bias_ref,
+    out_ref, spectrum_ref, turned_ref, column_ref, rows_ref, mixed_ref,
+):
+    turned_ref[...] = both_cells(jnp.transpose(local_ref[...].astype(F32)))
+    bias = jnp.transpose(jnp.broadcast_to(bias_ref[...], (128, C)))
+    column_ref[...] = jnp.concatenate([bias, bias], axis=0)
     spectrum = first_forward(in_ref[...], table_ref[...], FORWARD_FACTOR)
     spectrum_ref[...] = spectrum
     rows_ref[...] = jnp.zeros_like(rows_ref)
@@ -263,7 +302,9 @@
     out_ref[...] = first_inverse(modes * FORWARD_FACTOR, back_ref[...])
 
 
-def weight_grad_body(mine_ref, other_ref, out_ref, left_ref, right_ref):
+def weight_grad_body(
+    mine_ref, other_ref, pairs_ref, out_ref, act_ref, left_ref, right_ref, wide
+):
     left_ref[...] = jnp.zeros_like(left_ref)
     right_ref[...] = jnp.zeros_like(right_ref)
     for index, pack_ref in enumerate((mine_ref, other_ref)):
@@ -277,6 +318,12 @@
         out_ref[m * C : (m + 1) * C, :] = dot_rows(
             left_ref[rows, :], right_ref[rows, :], lax.Precision.HIGHEST
         )[:C]
+    for pair in range(2):
+        for y in range(8):
+            put_cell_pair(wide, y, pairs_ref[block(y, pair)].astype(F32))
+        act_ref[:, pair * 16 : (pair + 1) * 16, :] = (
+            wide[...].astype(BF16).reshape(C, 16, 128)
+        )
 
 
 ERFC = (
@@ -305,41 +352,44 @@
 
 
 def middle_body(
-    in_ref, local_ref, cot_ref, back_ref, table_ref, act_ref, grad_ref, out_ref, wide
+    in_ref, pairs_ref, cotangent_ref, weight_ref, column_ref, table_ref, act_ref, grad_ref,
+    out_ref, wide,
 ):
-    back = back_ref[...]
-    table = table_ref[...]
-
-    def step(y, carry):
-        for pair in range(2):
-            rows = pair_rows(y, pair)
-            pre = local_ref[rows, :] + dot_rows(stacked(depth_modes(in_ref, y, pair)), back)
+    weight = weight_ref[...]
+    bias = jnp.concatenate([column_ref[...]] * MIDDLE_GROUP, axis=0)
+    back = table_ref[DEPTH_BACK]
+    table = table_ref[DEPTH]
+    for pair in range(2):
+        part = cotangent_ref[:, pair * 16 : (pair + 1) * 16, :]
+        wide[...] = part.astype(F32).reshape(C * 16, 128)
+        for ys in y_groups(MIDDLE_GROUP):
+            pre = back_and_local(in_ref, back, weight, pairs_ref, ys, pair) + bias
             activation, slope = gelu_and_slope(pre)
-            put_cell_pair(wide, y, pair, activation)
-            grad_pre = (cot_ref[rows, :].astype(F32) * slope).astype(BF16)
-            grad_ref[rows, :] = grad_pre
-            send_depth(table, grad_pre, out_ref, y, pair)
-        return carry
-
-    lax.fori_loop(0, 8, step, 0)
-    act_ref[...] = wide[...].astype(BF16)
-
-
-def last_body(in_ref, grad_ref, weight_ref, back_ref, out_ref, wide):
-    back = back_ref[...]
-    weight = weight_ref[...]
-
-    def step(y, carry):
-        for pair in range(2):
-            cells = grad_ref[pair_rows(y, pair), :]
-            both = [dot(weight, cells[q * C : (q + 1) * C]) for q in range(2)]
-            total = jnp.concatenate(both, axis=0)
-            total += dot_rows(stacked(depth_modes(in_ref, y, pair)), back)
-            put_cell_pair(wide, y, pair, total)
-        return carry
-
-    lax.fori_loop(0, 8, step, 0)
-    out_ref[...] = wide[...].astype(BF16)
+            cotangent = jnp.concatenate([cell_pair(wide, y) for y in ys], axis=0)
+            activation = activation.astype(BF16)
+            grad_pre = (cotangent * slope).astype(BF16)
+            send_depth(table, grad_pre, out_ref, ys, pair)
+            for i, y in enumerate(ys):
+                act_ref[block(y, pair)] = activation[i * 128 : (i + 1) * 128]
+                grad_ref[block(y, pair)] = grad_pre[i * 128 : (i + 1) * 128]
+
+
+def last_body(in_ref, grad_ref, weight_ref, table_ref, out_ref, wide, cells_ref, sems):
+    back = table_ref[DEPTH_BACK]
+    weight = both_cells(weight_ref[...].astype(F32))
+    copies = []
+    for pair in range(2):
+        for ys in y_groups(LAST_GROUP):
+            total = back_and_local(in_ref, back, weight, grad_ref, ys, pair)
+            for i, y in enumerate(ys):
+                put_cell_pair(wide, y, total[i * 128 : (i + 1) * 128])
+        cells_ref[pair] = wide[...].astype(BF16).reshape(C, 16, 128)
+        copies.append(
+            pltpu.make_async_copy(cells_ref.at[pair], part_of(out_ref, pair), sems.at[pair])
+        )
+        copies[pair].start()
+    for copy in copies:
+        copy.wait()
 
 
 def over_py(values):
@@ -351,59 +401,69 @@
 
 
 def shards(fields, cotangent, spectral_weight, local_weight, bias_term):
-    depth_table, depth_back = depth_tables()
-    second_table, second_back = second_tables()
+    small = small_tables()
     first_table, first_back = first_tables()
     weight = spectral_weight.reshape(MODES * C, 128)
-    wide = pltpu.VMEM((C * CELLS, 128), F32)
+    wide = pltpu.VMEM((C * 16, 128), F32)
+    halves_of_cells = pltpu.VMEM((2, C, 16, 128), BF16)
     rows = pltpu.VMEM((MODES * 8, 128), F32)
     cells = C * CELLS
+    grid = jax.ShapeDtypeStruct((C, CELLS, 128), BF16)
+    in_place = pl.BlockSpec(memory_space=pltpu.HBM)
     second_forward = call(second_forward_body, shape(128), "y_forward")
     second_inverse = call(
         second_inverse_body, jax.ShapeDtypeStruct((PY, 64, 128), F32), "y_inverse"
     )
 
-    pairs, sent = call(depth_body, (shape(cells, BF16), shape(512)), "z_forward", [wide])(
-        fields.reshape(cells, 128), depth_table
-    )
-    received = over_py(sent)
-    local, cot = call(
-        local_body,
-        (shape(cells), shape(cells, BF16)),
-        "local_mix",
+    pairs, sent = call(
+        depth_body,
+        (shape(256, BF16, 1024), shape(512)),
+        "z_forward",
         [wide],
-        flops=2 * C * cells * 128,
-        nbytes=5 * cells * 256,
-    )(
-        pairs,
-        cotangent.reshape(cells, 128),
-        jnp.transpose(local_weight),
-        bias_term.reshape(C, 1),
-    )
-    received = over_px(second_forward(received, second_table))
-    sent, spectrum = call(mix_body, (shape(128), shape(64)), "modes_mix", [rows, rows])(
-        received, weight, first_table, first_back
-    )
-    received = over_py(second_inverse(over_px(sent), second_back))
+    )(fields.reshape(C, CELLS, 128))
+    received = over_px(second_forward(over_py(sent), small))
+    sent, spectrum, turned, column = call(
+        mix_body,
+        (shape(128), shape(64), shape(128, BF16), shape(128)),
+        "modes_mix",
+        [rows, rows],
+    )(received, weight, first_table, first_back, local_weight, bias_term.reshape(1, C))
+    received = over_py(second_inverse(over_px(sent), small))
     activation, grad_pre, sent = call(
         middle_body,
-        (shape(cells, BF16), shape(cells, BF16), shape(512)),
+        (shape(256, BF16, 1024), shape(256, BF16, 1024), shape(512)),
         "gelu_z",
         [wide],
-    )(received.reshape(512, 128), local, cot, depth_back, depth_table)
-    received = over_px(second_forward(over_py(sent), second_table))
+    )(
+        received.reshape(512, 128),
+        pairs,
+        cotangent.reshape(C, CELLS, 128),
+        turned,
+        column,
+        small,
+    )
+    received = over_px(second_forward(over_py(sent), small))
     sent, pack = call(mix_back_body, (shape(128), shape(128)), "modes_back", [rows, rows])(
         received, weight, spectrum, first_table, first_back
     )
     received = over_px(sent)
     other = lax.ppermute(pack, "pair", [(0, 1), (1, 0)])
-    weight_grad = call(
-        weight_grad_body, shape(MODES * C), "weight_grad", [rows, rows], flops=10**8, nbytes=10**6
-    )(pack, other)
-    received = over_py(second_inverse(received, second_back))
-    input_grad = call(last_body, shape(cells, BF16), "z_inverse", [wide])(
-        received.reshape(512, 128), grad_pre, local_weight, depth_back
-    )
+    weight_grad, activation = call(
+        weight_grad_body,
+        (shape(MODES * C), grid),
+        "weight_grad",
+        [rows, rows, wide],
+        flops=10**8,
+        nbytes=10**6,
+    )(pack, other, activation)
+    received = over_py(second_inverse(received, small))
+    input_grad = call(
+        last_body,
+        grid,
+        "z_inverse",
+        [wide, halves_of_cells, pltpu.SemaphoreType.DMA((2,))],
+        out_specs=in_place,
+    )(received.reshape(512, 128), grad_pre, local_weight, small)
     return (
         activation.reshape(fields.shape),
         input_grad.reshape(fields.shape),

time: 127 us -> 117 us (0.921)
  blocking collectives: 79.6 us -> 92.3 us
  Pallas kernels: 19.2 us -> 11 us
  waiting for transfers between devices: 13.7 us -> 6.91 us
  local copies, waits for them, and re-layouts: 5.43 us -> 1.72 us
  starting transfers between devices: 7.05 us -> 3.51 us
    all_to_all x2 -> x3, blocking collectives: 33.3 us -> 46 us  [over_py(): return lax.all_to_all(values.reshape(PY, 64, 128), 'py', 0, 0, tiled=True)]
    pallas_call x10 -> x9, Pallas kernels: 18.2 us -> 10 us  [the longest x1 3.37 us: shards(): call(weight_grad_body, (shape(MODES * C), grid), 'weight_grad', [rows, ro...]
    all_to_all x2 -> x1, waiting for transfers between devices: 12.5 us -> 5.67 us  [over_py(): return lax.all_to_all(values.reshape(PY, 64, 128), 'py', 0, 0, tiled=True)]
    unnamed x37 -> x16, local copies, waits for them, and re-layouts: 5.33 us -> 1.72 us
    all_to_all x2 -> x1, starting transfers between devices: 6.96 us -> 3.41 us  [over_py(): return lax.all_to_all(values.reshape(PY, 64, 128), 'py', 0, 0, tiled=True)]
  transfers between devices with their start and end apart: 3 -> 2, of which waited for: 3 -> 2; matrix products, arithmetic and copies ran while one was open for 1% -> 0% of each run, Pallas kernels for 4% -> 3%
where the time goes in v1:
time: 117 us; the launch traced here: 116 us
  blocking collectives  92.3 us (79%)
  Pallas kernels  11 us (9%)
  waiting for transfers between devices  6.91 us (6%)
  starting transfers between devices  3.51 us (3%)
  local copies, waits for them, and re-layouts  1.72 us (1%)
    all_to_all x4, blocking collectives, over_px(): lax.all_to_all(values.reshape(PX, 8, 128), 'px', 0, 0, tiled=True)  46.3 us
    all_to_all x3, blocking collectives, over_py(): return lax.all_to_all(values.reshape(PY, 64, 128), 'py', 0, 0, tiled=True)  46 us
    all_to_all x1, waiting for transfers between devices, over_py(): return lax.all_to_all(values.reshape(PY, 64, 128), 'py', 0, 0, tiled=True)  5.67 us
    all_to_all x1, starting transfers between devices, over_py(): return lax.all_to_all(values.reshape(PY, 64, 128), 'py', 0, 0, tiled=True)  3.41 us
    pallas_call x1, Pallas kernels, shards(): call(weight_grad_body, (shape(MODES * C), grid), 'weight_grad', [rows, ro...  3.37 us
  transfers between devices with their start and end apart: 2, of which 2 were waited for; matrix products, arithmetic and copies ran while one was open for 0% of the time, Pallas kernels for 3%

profile of v1, /device:TPU:2, one launch (start us, length us, event | category | flops | bytes accessed | tf_op | source)
XLA Modules:
  0.0 116.2 jit_solution(5976867365199088743)
XLA Ops:
  0.6 0.0 copy-start.3
  0.6 1.0 copy-done.3
  1.7 0.7 z_forward.1
  2.3 0.0 copy-start
  2.4 0.0 copy-start.1
  2.4 20.3 %all_to_all.40.in_ref = f32[8,64,128]{2,1,0:T(8,128)S(1)} all-to-all(f32[8,64,128]{2,1,0:T(8,128)S(1)} %bitcast.31), channel_id=1, replica_groups=mesh['px'=16,'py'=8,'pair'=2] {'py'}, dimensions={0} | all-to-all | bytes 524288 | tf_op jit(solution)/shard_map/all_to_all | solution.py:396
  22.6 0.0 copy-done
  22.6 0.0 copy-start.5
  22.6 0.2 y_forward.2
  22.9 0.0 copy-start.4
  22.9 0.0 copy-start.6
  22.9 13.7 %all_to_all.41 = f32[16,8,128]{2,1,0:T(8,128)S(1)} all-to-all(f32[16,8,128]{2,1,0:T(8,128)S(1)} %bitcast.26), channel_id=1, replica_groups=mesh['px'=16,'py'=8,'pair'=2] {'px'}, dimensions={0} | all-to-all | bytes 131072 | tf_op jit(solution)/shard_map/all_to_all | solution.py:400
  36.6 0.0 copy-start.7
  36.6 0.0 copy-done.1
  36.6 0.0 copy-done.5
  36.6 0.0 copy-done.4
  36.6 0.0 copy-done.6
  36.7 0.6 copy-done.7
  37.3 0.8 modes_mix.1
  38.1 0.0 copy-start.2
  38.1 10.9 %all_to_all.42 = f32[16,8,128]{2,1,0:T(8,128)S(1)} all-to-all(f32[16,8,128]{2,1,0:T(8,128)S(1)} %bitcast.34), channel_id=1, replica_groups=mesh['px'=16,'py'=8,'pair'=2] {'px'}, dimensions={0} | all-to-all | bytes 131072 | tf_op jit(solution)/shard_map/all_to_all | solution.py:400
  49.1 0.2 y_inverse.2
  49.2 12.9 %all_to_all.43 = f32[8,64,128]{2,1,0:T(8,128)S(1)} all-to-all(f32[8,64,128]{2,1,0:T(8,128)S(1)} %y_inverse.2), channel_id=1, replica_groups=mesh['px'=16,'py'=8,'pair'=2] {'py'}, dimensions={0} | all-to-all | bytes 524288 | tf_op jit(solution)/shard_map/all_to_all | solution.py:396
  62.1 0.0 copy-done.2
  62.1 2.3 %gelu_z.1 = (bf16[256,1024]{1,0:T(8,128)(2,1)S(1)}, bf16[256,1024]{1,0:T(8,128)(2,1)S(1)}, f32[512,128]{1,0:T(8,128)S(1)}) custom-call(f32[512,128]{1,0:T(8,128)S(1)} %bitcast.22, bf16[256,1024]{1,0:T(8,128)(2,1)S(1)} %get-tuple-element.18.pairs_ref, bf16[64,32,128]{2,1,0:T(8,128)(2,1)S(1)} %bitcast.23, bf16[128,128]{1,0:T(8,128)(2,1)S(1)} %get-tuple-element.19.weight_ref, ...), custom_call_target="tpu_custom_call" | custom-call | tf_op jit(solution)/shard_map/gelu_z/pallas_call | solution.py:432
  64.4 12.9 %all_to_all.44.in_ref = f32[8,64,128]{2,1,0:T(8,128)S(1)} all-to-all(f32[8,64,128]{2,1,0:T(8,128)S(1)} %bitcast.30), channel_id=1, replica_groups=mesh['px'=16,'py'=8,'pair'=2] {'py'}, dimensions={0} | all-to-all | bytes 524288 | tf_op jit(solution)/shard_map/all_to_all | solution.py:396
  77.3 0.2 y_forward.3
  77.5 10.8 %all_to_all.45 = f32[16,8,128]{2,1,0:T(8,128)S(1)} all-to-all(f32[16,8,128]{2,1,0:T(8,128)S(1)} %bitcast.28), channel_id=1, replica_groups=mesh['px'=16,'py'=8,'pair'=2] {'px'}, dimensions={0} | all-to-all | bytes 131072 | tf_op jit(solution)/shard_map/all_to_all | solution.py:400
  88.3 0.9 modes_back.1
  89.3 10.8 %all_to_all.46 = f32[16,8,128]{2,1,0:T(8,128)S(1)} all-to-all(f32[16,8,128]{2,1,0:T(8,128)S(1)} %bitcast.33), channel_id=1, replica_groups=mesh['px'=16,'py'=8,'pair'=2] {'px'}, dimensions={0} | all-to-all | bytes 131072 | tf_op jit(solution)/shard_map/all_to_all | solution.py:400
  100.1 0.9 y_inverse.3
  101.0 3.4 %all-to-all-start.7 = ((f32[8,64,128]{2,1,0:T(8,128)}), f32[8,64,128]{2,1,0:T(8,128)S(1)}, u32[]{:S(2)}, u32[]{:S(2)}) async-start(f32[8,64,128]{2,1,0:T(8,128)} %y_inverse.3), calls=%async_computation.7 | async-start | bytes 524288 | tf_op jit(solution)/shard_map/all_to_all | solution.py:396
  104.4 0.1 collective-permute-start
  104.5 1.2 %collective-permute-done.other_ref = f32[128,128]{1,0:T(8,128)S(1)} collective-permute-done((f32[128,128]{1,0:T(8,128)S(1)}, f32[128,128]{1,0:T(8,128)S(1)}, u32[]{:S(2)}, u32[]{:S(2)}) %collective-permute-start) | collective-permute-done | bytes 65568 | tf_op jit(solution)/shard_map/ppermute | solution.py:450
  105.7 3.4 %weight_grad.1 = (f32[2048,128]{1,0:T(8,128)}, bf16[64,32,128]{2,1,0:T(8,128)(2,1)}) custom-call(f32[128,128]{1,0:T(8,128)S(1)} %get-tuple-element.23.mine_ref, f32[128,128]{1,0:T(8,128)S(1)} %collective-permute-done.other_ref, bf16[256,1024]{1,0:T(8,128)(2,1)S(1)} %get-tuple-element.24.pairs_ref), custom_call_target="tpu_custom_call" | custom-call | flops 100000000 | bytes 1000000 | tf_op jit(solution)/shard_map/weight_grad/pallas_call | solution.py:451
  109.1 5.7 %all-to-all-done.7 = f32[8,64,128]{2,1,0:T(8,128)S(1)} async-done(((f32[8,64,128]{2,1,0:T(8,128)}), f32[8,64,128]{2,1,0:T(8,128)S(1)}, u32[]{:S(2)}, u32[]{:S(2)}) %all-to-all-start.7) | async-done | bytes 262176 | tf_op jit(solution)/shard_map/all_to_all | solution.py:396
  114.8 1.4 %z_inverse.1 = bf16[64,32,128]{2,1,0:T(8,128)(2,1)} custom-call(f32[512,128]{1,0:T(8,128)S(1)} %bitcast.21, bf16[256,1024]{1,0:T(8,128)(2,1)S(1)} %get-tuple-element.27.grad_ref, bf16[64,64]{1,0:T(8,128)(2,1)S(1)} %copy-done.6, bf16[224,256]{1,0:T(8,128)(2,1)S(1)} %copy-done), custom_call_target="tpu_custom_call" | custom-call | tf_op jit(solution)/shard_map/z_inverse/pallas_call | solution.py:460
Async XLA Ops:
  0.6 1.0 copy-start.3
  2.3 20.3 %copy-start = (bf16[224,256]{1,0:T(8,128)(2,1)S(1)}, bf16[224,256]{1,0:T(8,128)(2,1)}, u32[]{:S(2)}) copy-start(bf16[224,256]{1,0:T(8,128)(2,1)} %constant.6.clone.table_ref) | copy-start | bytes 344068
  2.4 34.3 %copy-start.1 = (bf16[1,2,16,64,128]{4,3,2,1,0:T(8,128)(2,1)S(1)}, bf16[1,2,16,64,128]{4,3,2,1,0:T(8,128)(2,1)}, u32[]{:S(2)}) copy-start(bf16[1,2,16,64,128]{4,3,2,1,0:T(8,128)(2,1)} %param.10) | copy-start | bytes 1572868
  22.6 14.0 %copy-start.5 = (bf16[128,384]{1,0:T(8,128)(2,1)S(1)}, bf16[128,384]{1,0:T(8,128)(2,1)}, u32[]{:S(2)}) copy-start(bf16[128,384]{1,0:T(8,128)(2,1)} %constant.7.clone.table_ref) | copy-start | bytes 294916
  22.9 13.8 %copy-start.4 = (bf16[128,384]{1,0:T(8,128)(2,1)S(1)}, bf16[128,384]{1,0:T(8,128)(2,1)}, u32[]{:S(2)}) copy-start(bf16[128,384]{1,0:T(8,128)(2,1)} %constant.8.clone.back_ref) | copy-start | bytes 294916
  22.9 13.7 %copy-start.6 = (bf16[64,64]{1,0:T(8,128)(2,1)S(1)}, bf16[64,64]{1,0:T(8,128)(2,1)}, u32[]{:S(2)}) copy-start(bf16[64,64]{1,0:T(8,128)(2,1)} %weight_ref.1) | copy-start | bytes 24580
  36.6 0.7 copy-start.7
  38.1 24.0 %copy-start.2 = (bf16[1,64,4,8,128]{4,3,2,1,0:T(8,128)(2,1)S(1)}, bf16[1,64,4,8,128]{4,3,2,1,0:T(8,128)(2,1)}, u32[]{:S(2)}) copy-start(bf16[1,64,4,8,128]{4,3,2,1,0:T(8,128)(2,1)} %param.9) | copy-start | bytes 1572868
  101.0 13.8 %all-to-all-start.7 = ((f32[8,64,128]{2,1,0:T(8,128)}), f32[8,64,128]{2,1,0:T(8,128)S(1)}, u32[]{:S(2)}, u32[]{:S(2)}) async-start(f32[8,64,128]{2,1,0:T(8,128)} %y_inverse.3), calls=%async_computation.7 | async-start | bytes 524288 | tf_op jit(solution)/shard_map/all_to_all | solution.py:396
  104.4 1.3 %collective-permute-start = (f32[128,128]{1,0:T(8,128)S(1)}, f32[128,128]{1,0:T(8,128)S(1)}, u32[]{:S(2)}, u32[]{:S(2)}) collective-permute-start(f32[128,128]{1,0:T(8,128)S(1)} %get-tuple-element.23.mine_ref), channel_id=1, source_target_pairs={{0,1},{1,0},{2,3},{3,2},{4,5},{5,4},{6,7},{7,6},{8,9},{9,8},{10,11... | collective-permute-start | bytes 196616 | tf_op jit(solution)/shard_map/ppermute | solution.py:450

commit v2 on v1

--- a/solution.py
+++ b/solution.py
@@ -24,6 +24,7 @@
 INVERSE_FACTOR = 1.0 / math.sqrt(KX * KY * KZ)
 F32 = jnp.float32
 BF16 = jnp.bfloat16
+PY_ORDER = (0, 4, 7, 3, 1, 5, 6, 2)
 MIDDLE_GROUP = 1
 LAST_GROUP = 1
 
@@ -48,7 +49,7 @@
 
 def depth_tables():
     cosine, sine = cos_sin(NZ, KZ, NZ)
-    order = np.arange(KZ).reshape(PY, KZ // PY).T.reshape(-1)
+    order = np.array([2 * peer + kz for kz in range(2) for peer in PY_ORDER])
     forward = np.concatenate([cosine.T[order], -sine.T[order]], axis=0)
     backward = np.concatenate([cosine.T[order], -sine.T[order]], axis=0)
     forward = forward.astype(np.float32).astype(ml_dtypes.bfloat16)
@@ -57,6 +58,8 @@
 
 def second_tables():
     cosine, sine = cos_sin(NY, KY, NY)
+    cells = np.array([8 * peer + cell for peer in PY_ORDER for cell in range(8)])
+    cosine, sine = cosine[cells], sine[cells]
     forward = np.concatenate([cosine.T, sine.T], axis=0)
     backward = np.concatenate([cosine, sine], axis=1)
     return stacked_table(forward, 1), stacked_table(backward, 1)
@@ -182,7 +185,8 @@
 def depth_table_here():
     row = lax.broadcasted_iota(jnp.int32, (32, 128), 0)
     cell = lax.broadcasted_iota(jnp.int32, (32, 128), 1)
-    wave = 2 * (row % 8) + (row // 8) % 2
+    peer = sum(jnp.where(row % 8 == slot, peer, 0) for slot, peer in enumerate(PY_ORDER))
+    wave = 2 * peer + (row // 8) % 2
     phase = (wave * cell + (NZ // 4) * (row // 16)) % NZ
     return jnp.cos(phase.astype(F32) * (2.0 * math.pi / NZ)).astype(BF16)
 
@@ -393,7 +397,9 @@
 
 
 def over_py(values):
-    return lax.all_to_all(values.reshape(PY, 64, 128), "py", 0, 0, tiled=True)
+    return lax.all_to_all(
+        values.reshape(PY, 64, 128), "py", 0, 0, tiled=True, axis_index_groups=[list(PY_ORDER)]
+    )
 
 
 def over_px(values):

time: 117 us -> 112 us (0.957)
  blocking collectives: 92.3 us -> 88.7 us
  waiting for transfers between devices: 6.91 us -> 5.06 us
    all_to_all x3, blocking collectives: 46 us -> 42.5 us  [over_py(): lax.all_to_all(values.reshape(PY, 64, 128), 'py', 0, 0, tiled=True, axis_...]
    all_to_all x1, waiting for transfers between devices: 5.67 us -> 3.81 us  [over_py(): lax.all_to_all(values.reshape(PY, 64, 128), 'py', 0, 0, tiled=True, axis_...]
where the time goes in v2:
time: 112 us; the launch traced here: 111 us
  blocking collectives  88.7 us (79%)
  Pallas kernels  11 us (10%)
  waiting for transfers between devices  5.06 us (5%)
  starting transfers between devices  3.89 us (3%)
  local copies, waits for them, and re-layouts  1.72 us (2%)
    all_to_all x4, blocking collectives, over_px(): lax.all_to_all(values.reshape(PX, 8, 128), 'px', 0, 0, tiled=True)  46.3 us
    all_to_all x3, blocking collectives, over_py(): lax.all_to_all(values.reshape(PY, 64, 128), 'py', 0, 0, tiled=True, axis_...  42.5 us
    all_to_all x1, starting transfers between devices, over_py(): lax.all_to_all(values.reshape(PY, 64, 128), 'py', 0, 0, tiled=True, axis_...  3.88 us
    all_to_all x1, waiting for transfers between devices, over_py(): lax.all_to_all(values.reshape(PY, 64, 128), 'py', 0, 0, tiled=True, axis_...  3.81 us
    pallas_call x1, Pallas kernels, shards(): call(weight_grad_body, (shape(MODES * C), grid), 'weight_grad', [rows, ro...  3.37 us
    pallas_call x1, Pallas kernels, shards(): call(middle_body, (shape(256, BF16, 1024), shape(256, BF16, 1024), shape(...  2.25 us
  transfers between devices with their start and end apart: 2, of which 2 were waited for; matrix products, arithmetic and copies ran while one was open for 0% of the time, Pallas kernels for 3%

profile of v2, /device:TPU:2, one launch (start us, length us, event | category | flops | bytes accessed | tf_op | source)
XLA Modules:
  0.0 111.1 jit_solution(12614568621625044540)
XLA Ops:
  0.6 0.0 copy-start.3
  0.6 1.0 copy-done.3
  1.7 0.7 z_forward.1
  2.4 0.0 copy-start
  2.4 0.0 copy-start.1
  2.4 18.3 %all_to_all.40.in_ref = f32[8,64,128]{2,1,0:T(8,128)S(1)} all-to-all(f32[8,64,128]{2,1,0:T(8,128)S(1)} %bitcast.31), channel_id=1, replica_groups={{0,8,14,6,2,10,12,4},{1,9,15,7,3,11,13,5},{16,24,30,22,18,26,28,20},{17..., dimensions={0} | all-to-all | bytes 524288 | tf_op jit(solution)/shard_map/all_to_all | solution.py:400
  20.7 0.0 copy-done
  20.7 0.0 copy-start.5
  20.7 0.2 y_forward.2
  20.9 0.0 copy-start.4
  21.0 0.0 copy-start.6
  21.0 13.7 %all_to_all.41 = f32[16,8,128]{2,1,0:T(8,128)S(1)} all-to-all(f32[16,8,128]{2,1,0:T(8,128)S(1)} %bitcast.26), channel_id=1, replica_groups=mesh['px'=16,'py'=8,'pair'=2] {'px'}, dimensions={0} | all-to-all | bytes 131072 | tf_op jit(solution)/shard_map/all_to_all | solution.py:406
  34.7 0.0 copy-start.7
  34.7 0.0 copy-done.1
  34.7 0.0 copy-done.5
  34.7 0.0 copy-done.4
  34.7 0.0 copy-done.6
  34.7 0.6 copy-done.7
  35.3 0.8 modes_mix.1
  36.2 0.0 copy-start.2
  36.2 10.9 %all_to_all.42 = f32[16,8,128]{2,1,0:T(8,128)S(1)} all-to-all(f32[16,8,128]{2,1,0:T(8,128)S(1)} %bitcast.34), channel_id=1, replica_groups=mesh['px'=16,'py'=8,'pair'=2] {'px'}, dimensions={0} | all-to-all | bytes 131072 | tf_op jit(solution)/shard_map/all_to_all | solution.py:406
  47.1 0.2 y_inverse.2
  47.3 12.3 %all_to_all.43 = f32[8,64,128]{2,1,0:T(8,128)S(1)} all-to-all(f32[8,64,128]{2,1,0:T(8,128)S(1)} %y_inverse.2), channel_id=1, replica_groups={{0,8,14,6,2,10,12,4},{1,9,15,7,3,11,13,5},{16,24,30,22,18,26,28,20},{17..., dimensions={0} | all-to-all | bytes 524288 | tf_op jit(solution)/shard_map/all_to_all | solution.py:400
  59.6 0.0 copy-done.2
  59.6 2.3 %gelu_z.1 = (bf16[256,1024]{1,0:T(8,128)(2,1)S(1)}, bf16[256,1024]{1,0:T(8,128)(2,1)S(1)}, f32[512,128]{1,0:T(8,128)S(1)}) custom-call(f32[512,128]{1,0:T(8,128)S(1)} %bitcast.22, bf16[256,1024]{1,0:T(8,128)(2,1)S(1)} %get-tuple-element.18.pairs_ref, bf16[64,32,128]{2,1,0:T(8,128)(2,1)S(1)} %bitcast.23, bf16[128,128]{1,0:T(8,128)(2,1)S(1)} %get-tuple-element.19.weight_ref, ...), custom_call_target="tpu_custom_call" | custom-call | tf_op jit(solution)/shard_map/gelu_z/pallas_call | solution.py:438
  61.8 11.9 %all_to_all.44.in_ref = f32[8,64,128]{2,1,0:T(8,128)S(1)} all-to-all(f32[8,64,128]{2,1,0:T(8,128)S(1)} %bitcast.30), channel_id=1, replica_groups={{0,8,14,6,2,10,12,4},{1,9,15,7,3,11,13,5},{16,24,30,22,18,26,28,20},{17..., dimensions={0} | all-to-all | bytes 524288 | tf_op jit(solution)/shard_map/all_to_all | solution.py:400
  73.7 0.2 y_forward.3
  74.0 10.8 %all_to_all.45 = f32[16,8,128]{2,1,0:T(8,128)S(1)} all-to-all(f32[16,8,128]{2,1,0:T(8,128)S(1)} %bitcast.28), channel_id=1, replica_groups=mesh['px'=16,'py'=8,'pair'=2] {'px'}, dimensions={0} | all-to-all | bytes 131072 | tf_op jit(solution)/shard_map/all_to_all | solution.py:406
  84.8 0.9 modes_back.1
  85.7 10.8 %all_to_all.46 = f32[16,8,128]{2,1,0:T(8,128)S(1)} all-to-all(f32[16,8,128]{2,1,0:T(8,128)S(1)} %bitcast.33), channel_id=1, replica_groups=mesh['px'=16,'py'=8,'pair'=2] {'px'}, dimensions={0} | all-to-all | bytes 131072 | tf_op jit(solution)/shard_map/all_to_all | solution.py:406
  96.5 0.9 y_inverse.3
  97.4 3.9 %all-to-all-start.7 = ((f32[8,64,128]{2,1,0:T(8,128)}), f32[8,64,128]{2,1,0:T(8,128)S(1)}, u32[]{:S(2)}, u32[]{:S(2)}) async-start(f32[8,64,128]{2,1,0:T(8,128)} %y_inverse.3), calls=%async_computation.7 | async-start | bytes 524288 | tf_op jit(solution)/shard_map/all_to_all | solution.py:400
  101.3 0.0 collective-permute-start
  101.3 1.2 %collective-permute-done.other_ref = f32[128,128]{1,0:T(8,128)S(1)} collective-permute-done((f32[128,128]{1,0:T(8,128)S(1)}, f32[128,128]{1,0:T(8,128)S(1)}, u32[]{:S(2)}, u32[]{:S(2)}) %collective-permute-start) | collective-permute-done | bytes 65568 | tf_op jit(solution)/shard_map/ppermute | solution.py:456
  102.5 3.4 %weight_grad.1 = (f32[2048,128]{1,0:T(8,128)}, bf16[64,32,128]{2,1,0:T(8,128)(2,1)}) custom-call(f32[128,128]{1,0:T(8,128)S(1)} %get-tuple-element.23.mine_ref, f32[128,128]{1,0:T(8,128)S(1)} %collective-permute-done.other_ref, bf16[256,1024]{1,0:T(8,128)(2,1)S(1)} %get-tuple-element.24.pairs_ref), custom_call_target="tpu_custom_call" | custom-call | flops 100000000 | bytes 1000000 | tf_op jit(solution)/shard_map/weight_grad/pallas_call | solution.py:457
  105.9 3.8 %all-to-all-done.7 = f32[8,64,128]{2,1,0:T(8,128)S(1)} async-done(((f32[8,64,128]{2,1,0:T(8,128)}), f32[8,64,128]{2,1,0:T(8,128)S(1)}, u32[]{:S(2)}, u32[]{:S(2)}) %all-to-all-start.7) | async-done | bytes 262176 | tf_op jit(solution)/shard_map/all_to_all | solution.py:400
  109.7 1.4 %z_inverse.1 = bf16[64,32,128]{2,1,0:T(8,128)(2,1)} custom-call(f32[512,128]{1,0:T(8,128)S(1)} %bitcast.21, bf16[256,1024]{1,0:T(8,128)(2,1)S(1)} %get-tuple-element.27.grad_ref, bf16[64,64]{1,0:T(8,128)(2,1)S(1)} %copy-done.6, bf16[224,256]{1,0:T(8,128)(2,1)S(1)} %copy-done), custom_call_target="tpu_custom_call" | custom-call | tf_op jit(solution)/shard_map/z_inverse/pallas_call | solution.py:466
Async XLA Ops:
  0.6 1.0 copy-start.3
  2.4 18.3 %copy-start = (bf16[224,256]{1,0:T(8,128)(2,1)S(1)}, bf16[224,256]{1,0:T(8,128)(2,1)}, u32[]{:S(2)}) copy-start(bf16[224,256]{1,0:T(8,128)(2,1)} %constant.6.clone.table_ref) | copy-start | bytes 344068
  2.4 32.3 %copy-start.1 = (bf16[1,2,16,64,128]{4,3,2,1,0:T(8,128)(2,1)S(1)}, bf16[1,2,16,64,128]{4,3,2,1,0:T(8,128)(2,1)}, u32[]{:S(2)}) copy-start(bf16[1,2,16,64,128]{4,3,2,1,0:T(8,128)(2,1)} %param.10) | copy-start | bytes 1572868
  20.7 14.0 %copy-start.5 = (bf16[128,384]{1,0:T(8,128)(2,1)S(1)}, bf16[128,384]{1,0:T(8,128)(2,1)}, u32[]{:S(2)}) copy-start(bf16[128,384]{1,0:T(8,128)(2,1)} %constant.7.clone.table_ref) | copy-start | bytes 294916
  20.9 13.8 %copy-start.4 = (bf16[128,384]{1,0:T(8,128)(2,1)S(1)}, bf16[128,384]{1,0:T(8,128)(2,1)}, u32[]{:S(2)}) copy-start(bf16[128,384]{1,0:T(8,128)(2,1)} %constant.8.clone.back_ref) | copy-start | bytes 294916
  21.0 13.7 %copy-start.6 = (bf16[64,64]{1,0:T(8,128)(2,1)S(1)}, bf16[64,64]{1,0:T(8,128)(2,1)}, u32[]{:S(2)}) copy-start(bf16[64,64]{1,0:T(8,128)(2,1)} %weight_ref.1) | copy-start | bytes 24580
  34.7 0.7 copy-start.7
  36.2 23.4 %copy-start.2 = (bf16[1,64,4,8,128]{4,3,2,1,0:T(8,128)(2,1)S(1)}, bf16[1,64,4,8,128]{4,3,2,1,0:T(8,128)(2,1)}, u32[]{:S(2)}) copy-start(bf16[1,64,4,8,128]{4,3,2,1,0:T(8,128)(2,1)} %param.9) | copy-start | bytes 1572868
  97.4 12.3 %all-to-all-start.7 = ((f32[8,64,128]{2,1,0:T(8,128)}), f32[8,64,128]{2,1,0:T(8,128)S(1)}, u32[]{:S(2)}, u32[]{:S(2)}) async-start(f32[8,64,128]{2,1,0:T(8,128)} %y_inverse.3), calls=%async_computation.7 | async-start | bytes 524288 | tf_op jit(solution)/shard_map/all_to_all | solution.py:400
  101.3 1.3 %collective-permute-start = (f32[128,128]{1,0:T(8,128)S(1)}, f32[128,128]{1,0:T(8,128)S(1)}, u32[]{:S(2)}, u32[]{:S(2)}) collective-permute-start(f32[128,128]{1,0:T(8,128)S(1)} %get-tuple-element.23.mine_ref), channel_id=1, source_target_pairs={{0,1},{1,0},{2,3},{3,2},{4,5},{5,4},{6,7},{7,6},{8,9},{9,8},{10,11... | collective-permute-start | bytes 196616 | tf_op jit(solution)/shard_map/ppermute | solution.py:456

commit v3 on v2

--- a/solution.py
+++ b/solution.py
@@ -24,7 +24,7 @@
 INVERSE_FACTOR = 1.0 / math.sqrt(KX * KY * KZ)
 F32 = jnp.float32
 BF16 = jnp.bfloat16
-PY_ORDER = (0, 4, 7, 3, 1, 5, 6, 2)
+PY_ORDER = (6, 2, 5, 1, 7, 3, 4, 0)
 MIDDLE_GROUP = 1
 LAST_GROUP = 1
 

time: 112 us -> 111 us (level)
  starting transfers between devices: 3.89 us -> 6.21 us
  waiting for transfers between devices: 5.06 us -> 2.78 us
  blocking collectives: 88.7 us -> 87.2 us
    all_to_all x1, starting transfers between devices: 3.88 us -> 6.21 us  [over_py(): lax.all_to_all(values.reshape(PY, 64, 128), 'py', 0, 0, tiled=True, axis_...]
    all_to_all x1, waiting for transfers between devices: 3.81 us -> 1.53 us  [over_py(): lax.all_to_all(values.reshape(PY, 64, 128), 'py', 0, 0, tiled=True, axis_...]
    all_to_all x3, blocking collectives: 42.5 us -> 41 us  [over_py(): lax.all_to_all(values.reshape(PY, 64, 128), 'py', 0, 0, tiled=True, axis_...]
where the time goes in v3:
time: 111 us; the launch traced here: 110 us
  blocking collectives  87.2 us (79%)
  Pallas kernels  11 us (10%)
  starting transfers between devices  6.21 us (6%)
  waiting for transfers between devices  2.78 us (3%)
  local copies, waits for them, and re-layouts  1.72 us (2%)
    all_to_all x4, blocking collectives, over_px(): lax.all_to_all(values.reshape(PX, 8, 128), 'px', 0, 0, tiled=True)  46.3 us
    all_to_all x3, blocking collectives, over_py(): lax.all_to_all(values.reshape(PY, 64, 128), 'py', 0, 0, tiled=True, axis_...  41 us
    all_to_all x1, starting transfers between devices, over_py(): lax.all_to_all(values.reshape(PY, 64, 128), 'py', 0, 0, tiled=True, axis_...  6.21 us
    pallas_call x1, Pallas kernels, shards(): call(weight_grad_body, (shape(MODES * C), grid), 'weight_grad', [rows, ro...  3.37 us
    pallas_call x1, Pallas kernels, shards(): call(middle_body, (shape(256, BF16, 1024), shape(256, BF16, 1024), shape(...  2.25 us
  transfers between devices with their start and end apart: 2, of which 2 were waited for; matrix products, arithmetic and copies ran while one was open for 0% of the time, Pallas kernels for 3%

profile of v3, /device:TPU:2, one launch (start us, length us, event | category | flops | bytes accessed | tf_op | source)
XLA Modules:
  0.0 109.7 jit_solution(864932863210212874)
XLA Ops:
  0.6 0.0 copy-start.3
  0.6 1.0 copy-done.3
  1.7 0.7 z_forward.1
  2.4 0.0 copy-start
  2.4 0.0 copy-start.1
  2.4 16.6 %all_to_all.40.in_ref = f32[8,64,128]{2,1,0:T(8,128)S(1)} all-to-all(f32[8,64,128]{2,1,0:T(8,128)S(1)} %bitcast.31), channel_id=1, replica_groups={{12,4,10,2,14,6,8,0},{13,5,11,3,15,7,9,1},{28,20,26,18,30,22,24,16},{29..., dimensions={0} | all-to-all | bytes 524288 | tf_op jit(solution)/shard_map/all_to_all | solution.py:400
  18.9 0.0 copy-done
  19.0 0.0 copy-start.5
  19.0 0.2 y_forward.2
  19.2 0.0 copy-start.4
  19.2 0.0 copy-start.6
  19.2 13.7 %all_to_all.41 = f32[16,8,128]{2,1,0:T(8,128)S(1)} all-to-all(f32[16,8,128]{2,1,0:T(8,128)S(1)} %bitcast.26), channel_id=1, replica_groups=mesh['px'=16,'py'=8,'pair'=2] {'px'}, dimensions={0} | all-to-all | bytes 131072 | tf_op jit(solution)/shard_map/all_to_all | solution.py:406
  32.9 0.0 copy-start.7
  32.9 0.0 copy-done.1
  32.9 0.0 copy-done.5
  32.9 0.0 copy-done.4
  33.0 0.0 copy-done.6
  33.0 0.6 copy-done.7
  33.6 0.8 modes_mix.1
  34.4 0.0 copy-start.2
  34.4 10.9 %all_to_all.42 = f32[16,8,128]{2,1,0:T(8,128)S(1)} all-to-all(f32[16,8,128]{2,1,0:T(8,128)S(1)} %bitcast.34), channel_id=1, replica_groups=mesh['px'=16,'py'=8,'pair'=2] {'px'}, dimensions={0} | all-to-all | bytes 131072 | tf_op jit(solution)/shard_map/all_to_all | solution.py:406
  45.4 0.2 y_inverse.2
  45.6 12.2 %all_to_all.43 = f32[8,64,128]{2,1,0:T(8,128)S(1)} all-to-all(f32[8,64,128]{2,1,0:T(8,128)S(1)} %y_inverse.2), channel_id=1, replica_groups={{12,4,10,2,14,6,8,0},{13,5,11,3,15,7,9,1},{28,20,26,18,30,22,24,16},{29..., dimensions={0} | all-to-all | bytes 524288 | tf_op jit(solution)/shard_map/all_to_all | solution.py:400
  57.8 0.0 copy-done.2
  57.8 2.3 %gelu_z.1 = (bf16[256,1024]{1,0:T(8,128)(2,1)S(1)}, bf16[256,1024]{1,0:T(8,128)(2,1)S(1)}, f32[512,128]{1,0:T(8,128)S(1)}) custom-call(f32[512,128]{1,0:T(8,128)S(1)} %bitcast.22, bf16[256,1024]{1,0:T(8,128)(2,1)S(1)} %get-tuple-element.18.pairs_ref, bf16[64,32,128]{2,1,0:T(8,128)(2,1)S(1)} %bitcast.23, bf16[128,128]{1,0:T(8,128)(2,1)S(1)} %get-tuple-element.19.weight_ref, ...), custom_call_target="tpu_custom_call" | custom-call | tf_op jit(solution)/shard_map/gelu_z/pallas_call | solution.py:438
  60.0 12.2 %all_to_all.44.in_ref = f32[8,64,128]{2,1,0:T(8,128)S(1)} all-to-all(f32[8,64,128]{2,1,0:T(8,128)S(1)} %bitcast.30), channel_id=1, replica_groups={{12,4,10,2,14,6,8,0},{13,5,11,3,15,7,9,1},{28,20,26,18,30,22,24,16},{29..., dimensions={0} | all-to-all | bytes 524288 | tf_op jit(solution)/shard_map/all_to_all | solution.py:400
  72.2 0.2 y_forward.3
  72.5 10.8 %all_to_all.45 = f32[16,8,128]{2,1,0:T(8,128)S(1)} all-to-all(f32[16,8,128]{2,1,0:T(8,128)S(1)} %bitcast.28), channel_id=1, replica_groups=mesh['px'=16,'py'=8,'pair'=2] {'px'}, dimensions={0} | all-to-all | bytes 131072 | tf_op jit(solution)/shard_map/all_to_all | solution.py:406
  83.3 0.9 modes_back.1
  84.2 10.8 %all_to_all.46 = f32[16,8,128]{2,1,0:T(8,128)S(1)} all-to-all(f32[16,8,128]{2,1,0:T(8,128)S(1)} %bitcast.33), channel_id=1, replica_groups=mesh['px'=16,'py'=8,'pair'=2] {'px'}, dimensions={0} | all-to-all | bytes 131072 | tf_op jit(solution)/shard_map/all_to_all | solution.py:406
  95.0 0.9 y_inverse.3
  95.9 6.2 %all-to-all-start.7 = ((f32[8,64,128]{2,1,0:T(8,128)}), f32[8,64,128]{2,1,0:T(8,128)S(1)}, u32[]{:S(2)}, u32[]{:S(2)}) async-start(f32[8,64,128]{2,1,0:T(8,128)} %y_inverse.3), calls=%async_computation.7 | async-start | bytes 524288 | tf_op jit(solution)/shard_map/all_to_all | solution.py:400
  102.1 0.0 collective-permute-start
  102.1 1.3 %collective-permute-done.other_ref = f32[128,128]{1,0:T(8,128)S(1)} collective-permute-done((f32[128,128]{1,0:T(8,128)S(1)}, f32[128,128]{1,0:T(8,128)S(1)}, u32[]{:S(2)}, u32[]{:S(2)}) %collective-permute-start) | collective-permute-done | bytes 65568 | tf_op jit(solution)/shard_map/ppermute | solution.py:456
  103.4 3.4 %weight_grad.1 = (f32[2048,128]{1,0:T(8,128)}, bf16[64,32,128]{2,1,0:T(8,128)(2,1)}) custom-call(f32[128,128]{1,0:T(8,128)S(1)} %get-tuple-element.23.mine_ref, f32[128,128]{1,0:T(8,128)S(1)} %collective-permute-done.other_ref, bf16[256,1024]{1,0:T(8,128)(2,1)S(1)} %get-tuple-element.24.pairs_ref), custom_call_target="tpu_custom_call" | custom-call | flops 100000000 | bytes 1000000 | tf_op jit(solution)/shard_map/weight_grad/pallas_call | solution.py:457
  106.8 1.5 %all-to-all-done.7 = f32[8,64,128]{2,1,0:T(8,128)S(1)} async-done(((f32[8,64,128]{2,1,0:T(8,128)}), f32[8,64,128]{2,1,0:T(8,128)S(1)}, u32[]{:S(2)}, u32[]{:S(2)}) %all-to-all-start.7) | async-done | bytes 262176 | tf_op jit(solution)/shard_map/all_to_all | solution.py:400
  108.3 1.4 %z_inverse.1 = bf16[64,32,128]{2,1,0:T(8,128)(2,1)} custom-call(f32[512,128]{1,0:T(8,128)S(1)} %bitcast.21, bf16[256,1024]{1,0:T(8,128)(2,1)S(1)} %get-tuple-element.27.grad_ref, bf16[64,64]{1,0:T(8,128)(2,1)S(1)} %copy-done.6, bf16[224,256]{1,0:T(8,128)(2,1)S(1)} %copy-done), custom_call_target="tpu_custom_call" | custom-call | tf_op jit(solution)/shard_map/z_inverse/pallas_call | solution.py:466
Async XLA Ops:
  0.6 1.0 copy-start.3
  2.4 16.6 %copy-start = (bf16[224,256]{1,0:T(8,128)(2,1)S(1)}, bf16[224,256]{1,0:T(8,128)(2,1)}, u32[]{:S(2)}) copy-start(bf16[224,256]{1,0:T(8,128)(2,1)} %constant.6.clone.table_ref) | copy-start | bytes 344068
  2.4 30.6 %copy-start.1 = (bf16[1,2,16,64,128]{4,3,2,1,0:T(8,128)(2,1)S(1)}, bf16[1,2,16,64,128]{4,3,2,1,0:T(8,128)(2,1)}, u32[]{:S(2)}) copy-start(bf16[1,2,16,64,128]{4,3,2,1,0:T(8,128)(2,1)} %param.10) | copy-start | bytes 1572868
  19.0 14.0 %copy-start.5 = (bf16[128,384]{1,0:T(8,128)(2,1)S(1)}, bf16[128,384]{1,0:T(8,128)(2,1)}, u32[]{:S(2)}) copy-start(bf16[128,384]{1,0:T(8,128)(2,1)} %constant.7.clone.table_ref) | copy-start | bytes 294916
  19.2 13.8 %copy-start.4 = (bf16[128,384]{1,0:T(8,128)(2,1)S(1)}, bf16[128,384]{1,0:T(8,128)(2,1)}, u32[]{:S(2)}) copy-start(bf16[128,384]{1,0:T(8,128)(2,1)} %constant.8.clone.back_ref) | copy-start | bytes 294916
  19.2 13.7 %copy-start.6 = (bf16[64,64]{1,0:T(8,128)(2,1)S(1)}, bf16[64,64]{1,0:T(8,128)(2,1)}, u32[]{:S(2)}) copy-start(bf16[64,64]{1,0:T(8,128)(2,1)} %weight_ref.1) | copy-start | bytes 24580
  32.9 0.7 copy-start.7
  34.4 23.3 %copy-start.2 = (bf16[1,64,4,8,128]{4,3,2,1,0:T(8,128)(2,1)S(1)}, bf16[1,64,4,8,128]{4,3,2,1,0:T(8,128)(2,1)}, u32[]{:S(2)}) copy-start(bf16[1,64,4,8,128]{4,3,2,1,0:T(8,128)(2,1)} %param.9) | copy-start | bytes 1572868
  95.9 12.4 %all-to-all-start.7 = ((f32[8,64,128]{2,1,0:T(8,128)}), f32[8,64,128]{2,1,0:T(8,128)S(1)}, u32[]{:S(2)}, u32[]{:S(2)}) async-start(f32[8,64,128]{2,1,0:T(8,128)} %y_inverse.3), calls=%async_computation.7 | async-start | bytes 524288 | tf_op jit(solution)/shard_map/all_to_all | solution.py:400
  102.1 1.3 %collective-permute-start = (f32[128,128]{1,0:T(8,128)S(1)}, f32[128,128]{1,0:T(8,128)S(1)}, u32[]{:S(2)}, u32[]{:S(2)}) collective-permute-start(f32[128,128]{1,0:T(8,128)S(1)} %get-tuple-element.23.mine_ref), channel_id=1, source_target_pairs={{0,1},{1,0},{2,3},{3,2},{4,5},{5,4},{6,7},{7,6},{8,9},{9,8},{10,11... | collective-permute-start | bytes 196616 | tf_op jit(solution)/shard_map/ppermute | solution.py:456

commit v4 on v3

--- a/solution.py
+++ b/solution.py
@@ -24,7 +24,7 @@
 INVERSE_FACTOR = 1.0 / math.sqrt(KX * KY * KZ)
 F32 = jnp.float32
 BF16 = jnp.bfloat16
-PY_ORDER = (6, 2, 5, 1, 7, 3, 4, 0)
+PY_ORDER = (7, 3, 6, 2, 0, 4, 5, 1)
 MIDDLE_GROUP = 1
 LAST_GROUP = 1
 

time: 111 us -> 111 us (level)
  no operation moved by 1% of the time
where the time goes in v4:
time: 111 us; the launch traced here: 109 us
  blocking collectives  87 us (78%)
  Pallas kernels  11 us (10%)
  starting transfers between devices  6.17 us (6%)
  waiting for transfers between devices  2.78 us (3%)
  local copies, waits for them, and re-layouts  1.72 us (2%)
    all_to_all x4, blocking collectives, over_px(): lax.all_to_all(values.reshape(PX, 8, 128), 'px', 0, 0, tiled=True)  46.3 us
    all_to_all x3, blocking collectives, over_py(): lax.all_to_all(values.reshape(PY, 64, 128), 'py', 0, 0, tiled=True, axis_...  40.8 us
    all_to_all x1, starting transfers between devices, over_py(): lax.all_to_all(values.reshape(PY, 64, 128), 'py', 0, 0, tiled=True, axis_...  6.17 us
    pallas_call x1, Pallas kernels, shards(): call(weight_grad_body, (shape(MODES * C), grid), 'weight_grad', [rows, ro...  3.37 us
    pallas_call x1, Pallas kernels, shards(): call(middle_body, (shape(256, BF16, 1024), shape(256, BF16, 1024), shape(...  2.25 us
  transfers between devices with their start and end apart: 2, of which 2 were waited for; matrix products, arithmetic and copies ran while one was open for 0% of the time, Pallas kernels for 3%

profile of v4, /device:TPU:2, one launch (start us, length us, event | category | flops | bytes accessed | tf_op | source)
XLA Modules:
  0.0 109.5 jit_solution(10029590599265296855)
XLA Ops:
  0.6 0.0 copy-start.3
  0.6 1.0 copy-done.3
  1.7 0.7 z_forward.1
  2.4 0.0 copy-start
  2.4 0.0 copy-start.1
  2.4 16.2 %all_to_all.40.in_ref = f32[8,64,128]{2,1,0:T(8,128)S(1)} all-to-all(f32[8,64,128]{2,1,0:T(8,128)S(1)} %bitcast.31), channel_id=1, replica_groups={{14,6,12,4,0,8,10,2},{15,7,13,5,1,9,11,3},{30,22,28,20,16,24,26,18},{31..., dimensions={0} | all-to-all | bytes 524288 | tf_op jit(solution)/shard_map/all_to_all | solution.py:400
  18.6 0.0 copy-done
  18.6 0.0 copy-start.5
  18.6 0.2 y_forward.2
  18.8 0.0 copy-start.4
  18.8 0.0 copy-start.6
  18.8 13.7 %all_to_all.41 = f32[16,8,128]{2,1,0:T(8,128)S(1)} all-to-all(f32[16,8,128]{2,1,0:T(8,128)S(1)} %bitcast.26), channel_id=1, replica_groups=mesh['px'=16,'py'=8,'pair'=2] {'px'}, dimensions={0} | all-to-all | bytes 131072 | tf_op jit(solution)/shard_map/all_to_all | solution.py:406
  32.5 0.0 copy-start.7
  32.6 0.0 copy-done.1
  32.6 0.0 copy-done.5
  32.6 0.0 copy-done.4
  32.6 0.0 copy-done.6
  32.6 0.6 copy-done.7
  33.2 0.8 modes_mix.1
  34.0 0.0 copy-start.2
  34.0 10.9 %all_to_all.42 = f32[16,8,128]{2,1,0:T(8,128)S(1)} all-to-all(f32[16,8,128]{2,1,0:T(8,128)S(1)} %bitcast.34), channel_id=1, replica_groups=mesh['px'=16,'py'=8,'pair'=2] {'px'}, dimensions={0} | all-to-all | bytes 131072 | tf_op jit(solution)/shard_map/all_to_all | solution.py:406
  45.0 0.2 y_inverse.2
  45.2 12.5 %all_to_all.43 = f32[8,64,128]{2,1,0:T(8,128)S(1)} all-to-all(f32[8,64,128]{2,1,0:T(8,128)S(1)} %y_inverse.2), channel_id=1, replica_groups={{14,6,12,4,0,8,10,2},{15,7,13,5,1,9,11,3},{30,22,28,20,16,24,26,18},{31..., dimensions={0} | all-to-all | bytes 524288 | tf_op jit(solution)/shard_map/all_to_all | solution.py:400
  57.7 0.0 copy-done.2
  57.7 2.3 %gelu_z.1 = (bf16[256,1024]{1,0:T(8,128)(2,1)S(1)}, bf16[256,1024]{1,0:T(8,128)(2,1)S(1)}, f32[512,128]{1,0:T(8,128)S(1)}) custom-call(f32[512,128]{1,0:T(8,128)S(1)} %bitcast.22, bf16[256,1024]{1,0:T(8,128)(2,1)S(1)} %get-tuple-element.18.pairs_ref, bf16[64,32,128]{2,1,0:T(8,128)(2,1)S(1)} %bitcast.23, bf16[128,128]{1,0:T(8,128)(2,1)S(1)} %get-tuple-element.19.weight_ref, ...), custom_call_target="tpu_custom_call" | custom-call | tf_op jit(solution)/shard_map/gelu_z/pallas_call | solution.py:438
  59.9 12.1 %all_to_all.44.in_ref = f32[8,64,128]{2,1,0:T(8,128)S(1)} all-to-all(f32[8,64,128]{2,1,0:T(8,128)S(1)} %bitcast.30), channel_id=1, replica_groups={{14,6,12,4,0,8,10,2},{15,7,13,5,1,9,11,3},{30,22,28,20,16,24,26,18},{31..., dimensions={0} | all-to-all | bytes 524288 | tf_op jit(solution)/shard_map/all_to_all | solution.py:400
  72.0 0.2 y_forward.3
  72.3 10.8 %all_to_all.45 = f32[16,8,128]{2,1,0:T(8,128)S(1)} all-to-all(f32[16,8,128]{2,1,0:T(8,128)S(1)} %bitcast.28), channel_id=1, replica_groups=mesh['px'=16,'py'=8,'pair'=2] {'px'}, dimensions={0} | all-to-all | bytes 131072 | tf_op jit(solution)/shard_map/all_to_all | solution.py:406
  83.1 0.9 modes_back.1
  84.0 10.8 %all_to_all.46 = f32[16,8,128]{2,1,0:T(8,128)S(1)} all-to-all(f32[16,8,128]{2,1,0:T(8,128)S(1)} %bitcast.33), channel_id=1, replica_groups=mesh['px'=16,'py'=8,'pair'=2] {'px'}, dimensions={0} | all-to-all | bytes 131072 | tf_op jit(solution)/shard_map/all_to_all | solution.py:406
  94.8 0.9 y_inverse.3
  95.7 6.2 %all-to-all-start.7 = ((f32[8,64,128]{2,1,0:T(8,128)}), f32[8,64,128]{2,1,0:T(8,128)S(1)}, u32[]{:S(2)}, u32[]{:S(2)}) async-start(f32[8,64,128]{2,1,0:T(8,128)} %y_inverse.3), calls=%async_computation.7 | async-start | bytes 524288 | tf_op jit(solution)/shard_map/all_to_all | solution.py:400
  101.9 0.0 collective-permute-start
  101.9 1.3 %collective-permute-done.other_ref = f32[128,128]{1,0:T(8,128)S(1)} collective-permute-done((f32[128,128]{1,0:T(8,128)S(1)}, f32[128,128]{1,0:T(8,128)S(1)}, u32[]{:S(2)}, u32[]{:S(2)}) %collective-permute-start) | collective-permute-done | bytes 65568 | tf_op jit(solution)/shard_map/ppermute | solution.py:456
  103.2 3.4 %weight_grad.1 = (f32[2048,128]{1,0:T(8,128)}, bf16[64,32,128]{2,1,0:T(8,128)(2,1)}) custom-call(f32[128,128]{1,0:T(8,128)S(1)} %get-tuple-element.23.mine_ref, f32[128,128]{1,0:T(8,128)S(1)} %collective-permute-done.other_ref, bf16[256,1024]{1,0:T(8,128)(2,1)S(1)} %get-tuple-element.24.pairs_ref), custom_call_target="tpu_custom_call" | custom-call | flops 100000000 | bytes 1000000 | tf_op jit(solution)/shard_map/weight_grad/pallas_call | solution.py:457
  106.5 1.5 %all-to-all-done.7 = f32[8,64,128]{2,1,0:T(8,128)S(1)} async-done(((f32[8,64,128]{2,1,0:T(8,128)}), f32[8,64,128]{2,1,0:T(8,128)S(1)}, u32[]{:S(2)}, u32[]{:S(2)}) %all-to-all-start.7) | async-done | bytes 262176 | tf_op jit(solution)/shard_map/all_to_all | solution.py:400
  108.1 1.4 %z_inverse.1 = bf16[64,32,128]{2,1,0:T(8,128)(2,1)} custom-call(f32[512,128]{1,0:T(8,128)S(1)} %bitcast.21, bf16[256,1024]{1,0:T(8,128)(2,1)S(1)} %get-tuple-element.27.grad_ref, bf16[64,64]{1,0:T(8,128)(2,1)S(1)} %copy-done.6, bf16[224,256]{1,0:T(8,128)(2,1)S(1)} %copy-done), custom_call_target="tpu_custom_call" | custom-call | tf_op jit(solution)/shard_map/z_inverse/pallas_call | solution.py:466
Async XLA Ops:
  0.6 1.0 copy-start.3
  2.4 16.2 %copy-start = (bf16[224,256]{1,0:T(8,128)(2,1)S(1)}, bf16[224,256]{1,0:T(8,128)(2,1)}, u32[]{:S(2)}) copy-start(bf16[224,256]{1,0:T(8,128)(2,1)} %constant.6.clone.table_ref) | copy-start | bytes 344068
  2.4 30.2 %copy-start.1 = (bf16[1,2,16,64,128]{4,3,2,1,0:T(8,128)(2,1)S(1)}, bf16[1,2,16,64,128]{4,3,2,1,0:T(8,128)(2,1)}, u32[]{:S(2)}) copy-start(bf16[1,2,16,64,128]{4,3,2,1,0:T(8,128)(2,1)} %param.10) | copy-start | bytes 1572868
  18.6 14.0 %copy-start.5 = (bf16[128,384]{1,0:T(8,128)(2,1)S(1)}, bf16[128,384]{1,0:T(8,128)(2,1)}, u32[]{:S(2)}) copy-start(bf16[128,384]{1,0:T(8,128)(2,1)} %constant.7.clone.table_ref) | copy-start | bytes 294916
  18.8 13.8 %copy-start.4 = (bf16[128,384]{1,0:T(8,128)(2,1)S(1)}, bf16[128,384]{1,0:T(8,128)(2,1)}, u32[]{:S(2)}) copy-start(bf16[128,384]{1,0:T(8,128)(2,1)} %constant.8.clone.back_ref) | copy-start | bytes 294916
  18.8 13.7 %copy-start.6 = (bf16[64,64]{1,0:T(8,128)(2,1)S(1)}, bf16[64,64]{1,0:T(8,128)(2,1)}, u32[]{:S(2)}) copy-start(bf16[64,64]{1,0:T(8,128)(2,1)} %weight_ref.1) | copy-start | bytes 24580
  32.5 0.7 copy-start.7
  34.0 23.6 %copy-start.2 = (bf16[1,64,4,8,128]{4,3,2,1,0:T(8,128)(2,1)S(1)}, bf16[1,64,4,8,128]{4,3,2,1,0:T(8,128)(2,1)}, u32[]{:S(2)}) copy-start(bf16[1,64,4,8,128]{4,3,2,1,0:T(8,128)(2,1)} %param.9) | copy-start | bytes 1572868
  95.7 12.3 %all-to-all-start.7 = ((f32[8,64,128]{2,1,0:T(8,128)}), f32[8,64,128]{2,1,0:T(8,128)S(1)}, u32[]{:S(2)}, u32[]{:S(2)}) async-start(f32[8,64,128]{2,1,0:T(8,128)} %y_inverse.3), calls=%async_computation.7 | async-start | bytes 524288 | tf_op jit(solution)/shard_map/all_to_all | solution.py:400
  101.9 1.3 %collective-permute-start = (f32[128,128]{1,0:T(8,128)S(1)}, f32[128,128]{1,0:T(8,128)S(1)}, u32[]{:S(2)}, u32[]{:S(2)}) collective-permute-start(f32[128,128]{1,0:T(8,128)S(1)} %get-tuple-element.23.mine_ref), channel_id=1, source_target_pairs={{0,1},{1,0},{2,3},{3,2},{4,5},{5,4},{6,7},{7,6},{8,9},{9,8},{10,11... | collective-permute-start | bytes 196616 | tf_op jit(solution)/shard_map/ppermute | solution.py:456
